TPU v7x, 128 devices: a whole 4x4x4 slice. The times are simulated.
128 devices in a mesh: row: 8 (over z_hi, x), col: 16 (over y, z_lo, core).
Axes of the slice: x: 4, y: 4, z: 4 (z_hi: 2, z_lo: 2; z = z_hi * 2 + z_lo), core: 2. Of those that a mesh axis runs over, the one named last changes fastest.
Arguments:
- pair: float32 [768, 768, 128], P('row', 'col'), may hold values from -6 to 6
- in_gain: float32 [2, 128], replicated, may hold values from 0.1 to 1.9
- in_bias: float32 [2, 128], replicated, may hold values from -0.72 to 0.72
- mid_gain: float32 [2, 128], replicated, may hold values from 0.1 to 1.9
- mid_bias: float32 [2, 128], replicated, may hold values from -3 to 3
- w_in: bfloat16 [2, 128, 512], replicated, may hold values from -0.5 to 0.5
- w_gate: bfloat16 [2, 128, 128], replicated, may hold values from -0.5 to 0.5
- w_out: bfloat16 [2, 128, 128], replicated, may hold values from -0.5 to 0.5
Outputs:
- updated: float32 [768, 768, 128], P('row', 'col')
All inputs are finite; a program needn't handle non-finite values.
Results may differ from a plain program's by a relative error of at most 0.007.
Values may be sent and summed in bfloat16 or wider, within the bound.
A program may use at most 192 MiB of HBM per device.

v0:
```python
import jax
import jax.numpy as jnp
from jax import lax
from jax.sharding import PartitionSpec as P

epsilon = 1e-05


def layer_norm(values, gain_row, bias_row):
    centre = jnp.mean(values, axis=-1, keepdims=True)
    shifted = values - centre
    spread = jnp.mean(shifted * shifted, axis=-1, keepdims=True)
    return shifted * lax.rsqrt(spread + epsilon) * gain_row + bias_row


def inputs_of(pair_state, in_gain, in_bias, w_in, w_gate, layer_idx):
    normed = layer_norm(pair_state, in_gain[layer_idx], in_bias[layer_idx]).astype(jnp.bfloat16)
    projected = jnp.dot(normed, w_in[layer_idx], preferred_element_type=jnp.float32)
    width = w_in.shape[2] // 4
    left_act = (jax.nn.sigmoid(projected[..., :width]) * projected[..., width : 2 * width]).astype(
        jnp.bfloat16
    )
    right_act = (
        jax.nn.sigmoid(projected[..., 2 * width : 3 * width]) * projected[..., 3 * width :]
    ).astype(jnp.bfloat16)
    gate_act = jax.nn.sigmoid(
        jnp.dot(normed, w_gate[layer_idx], preferred_element_type=jnp.float32)
    )
    return (left_act, right_act, gate_act)


def finish(pair_state, tri_sum, gate_act, mid_gain, mid_bias, w_out, layer_idx):
    mixed_norm = layer_norm(tri_sum, mid_gain[layer_idx], mid_bias[layer_idx]).astype(jnp.bfloat16)
    return pair_state + gate_act * jnp.dot(
        mixed_norm, w_out[layer_idx], preferred_element_type=jnp.float32
    )


def local(pair, in_gain, in_bias, mid_gain, mid_bias, w_in, w_gate, w_out):
    left_act, right_act, gate_act = inputs_of(pair, in_gain, in_bias, w_in, w_gate, 0)
    rows_right = lax.all_gather(right_act, "row", axis=0, tiled=True)
    panel_part = rows_right
    summed = lax.psum_scatter(
        jnp.einsum("jkc,ikc->jic", panel_part, left_act, preferred_element_type=jnp.float32),
        "col",
        scatter_dimension=0,
        tiled=True,
    )
    tri_sum = jnp.transpose(summed, (1, 0, 2))
    after_out = finish(pair, tri_sum, gate_act, mid_gain, mid_bias, w_out, 0)
    left_act, right_act, gate_act = inputs_of(after_out, in_gain, in_bias, w_in, w_gate, 1)
    cols_left = lax.all_gather(left_act, "col", axis=1, tiled=True)
    panel_part = cols_left
    tri_sum = lax.psum_scatter(
        jnp.einsum(
            "kic,kjc->ijc", panel_part, right_act, preferred_element_type=jnp.float32
        ).astype(jnp.bfloat16),
        "row",
        scatter_dimension=0,
        tiled=True,
    ).astype(jnp.float32)
    return finish(after_out, tri_sum, gate_act, mid_gain, mid_bias, w_out, 1)


def solution(mesh):
    return jax.shard_map(
        local,
        mesh=mesh,
        in_specs=(P("row", "col", None), P(), P(), P(), P(), P(), P(), P()),
        out_specs=P("row", "col", None),
        check_vma=False,
    )
```

profile of v0, /device:TPU:1, one launch (start us, length us, event | category | flops | bytes accessed | tf_op | source)
XLA Modules:
  0.0 933.5 jit_solution(13785550851855271985)
XLA Ops:
  6.5 0.0 all-gather.3.cloned.1.call-start
  6.6 2.5 reduce_sum.72
  9.1 0.1 copy.60
  9.2 0.1 copy.61
  9.3 1.4 multiply_reduce_fusion.2
  10.7 0.1 copy.62
  10.8 0.1 copy.63
  10.9 0.0 copy-done.5
  11.0 0.6 copy-done.9
  11.5 1.4 fusion.30
  13.0 2.2 fusion.14
  15.2 0.0 all-gather.3.cloned.1.call-update
  15.3 0.0 reduce-scatter.3.cloned.1.call-start
  15.3 2.0 copy.64
  17.3 119.5 %all-gather.3.cloned.1.call-done = bf16[768,48,128]{2,1,0:T(8,128)(2,1)} async-done(((bf16[96,48,128]{2,1,0:T(8,128)(2,1)}), bf16[768,48,128]{2,1,0:T(8,128)(2,1)}) %all-gather.3.cloned.1.call-update) | async-done | bytes 9437200 | tf_op jit(solution)/shard_map/all_gather | solution.py:41
  136.8 14.0 %copy.65 = bf16[768,48,128]{0,1,2:T(8,128)(2,1)} copy(bf16[768,48,128]{2,1,0:T(8,128)(2,1)} %all-gather.3.cloned.1.call-done) | data formatting | bytes 18874368 | tf_op jit(solution)/shard_map/all_gather | solution.py:41
  150.7 21.7 %convolution_bitcast_fusion = f32[768,96,128]{0,1,2:T(8,128)} fusion(bf16[96,48,128]{0,1,2:T(8,128)(2,1)} %copy.64, bf16[768,48,128]{0,1,2:T(8,128)(2,1)} %copy.65), kind=kOutput, calls=%fused_computation | convolution fusion | flops 905969664 | bytes 48365568 | tf_op jit(solution)/shard_map/jkc,ikc->jic/dot_general | solution.py:44
  172.4 37.4 %copy.66 = f32[768,96,128]{2,1,0:T(8,128)} copy(f32[768,96,128]{0,1,2:T(8,128)} %convolution_bitcast_fusion) | data formatting | bytes 75497472 | tf_op jit(solution)/shard_map/jkc,ikc->jic/transpose | solution.py:44
  209.8 0.0 copy-start.15
  209.8 0.0 reduce-scatter.3.cloned.1.call-update
  209.8 0.2 all-gather.5.cloned.1.call-start
  210.1 0.4 copy-done.19
  210.5 0.0 copy-done.20
  210.5 0.6 slice_bitcast_fusion
  211.1 0.0 copy-done.10
  211.1 3.1 fusion.38
  214.2 385.5 %reduce-scatter.3.cloned.1.call-done = f32[48,96,128]{2,1,0:T(8,128)} async-done(((f32[768,96,128]{2,1,0:T(8,128)}), f32[48,96,128]{2,1,0:T(8,128)}) %reduce-scatter.3.cloned.1.call-update) | async-done | bytes 2359312 | tf_op jit(solution)/shard_map/reduce_scatter | solution.py:43
  599.7 2.7 bitcast_reduce_fusion
  602.4 1.7 multiply_reduce_fusion.1
  604.1 0.0 copy-start.4
  604.1 0.0 copy-start.23
  604.1 1.5 add_convert_fusion.1
  605.6 0.1 copy-done.4
  605.8 2.4 fusion.44
  608.2 0.1 copy.68
  608.2 0.1 copy.69
  608.3 2.8 multiply_reduce_fusion
  611.2 0.1 copy.70
  611.3 0.1 copy.71
  611.4 0.6 copy-done.11
  612.0 1.4 fusion.28
  613.4 2.2 fusion.6
  615.7 0.0 all-gather.5.cloned.1.call-update
  615.7 0.3 reduce-scatter.5.cloned.1.call-start
  616.0 2.0 copy.72
  618.0 99.9 %all-gather.5.cloned.1.call-done = bf16[96,768,128]{2,1,0:T(8,128)(2,1)} async-done(((bf16[96,48,128]{2,1,0:T(8,128)(2,1)}), bf16[96,768,128]{2,1,0:T(8,128)(2,1)}) %all-gather.5.cloned.1.call-update) | async-done | bytes 18874384 | tf_op jit(solution)/shard_map/all_gather | solution.py:52
  717.9 32.6 %copy.73 = bf16[96,768,128]{0,1,2:T(8,128)(2,1)} copy(bf16[96,768,128]{2,1,0:T(8,128)(2,1)} %all-gather.5.cloned.1.call-done) | data formatting | bytes 37748736 | tf_op jit(solution)/shard_map/all_gather | solution.py:52
  750.4 17.3 %convert_bitcast_fusion = bf16[768,48,128]{0,1,2:T(8,128)(2,1)} fusion(bf16[96,48,128]{0,1,2:T(8,128)(2,1)} %copy.72, bf16[96,768,128]{0,1,2:T(8,128)(2,1)} %copy.73), kind=kOutput, calls=%fused_computation.1 | convolution fusion | flops 910688256 | bytes 29491200 | tf_op jit(solution)/shard_map/kic,kjc->ijc/dot_general | solution.py:55
  767.8 14.0 %copy.74 = bf16[768,48,128]{2,1,0:T(8,128)(2,1)} copy(bf16[768,48,128]{0,1,2:T(8,128)(2,1)} %convert_bitcast_fusion) | data formatting | bytes 18874368 | tf_op jit(solution)/shard_map/convert_element_type | solution.py:57
  781.7 0.0 reduce-scatter.5.cloned.1.call-update
  781.8 0.8 copy-done.8
  782.5 0.0 copy-done.12
  782.5 0.1 copy-done.16
  782.6 3.1 fusion.35
  785.7 122.0 %reduce-scatter.5.cloned.1.call-done = bf16[96,48,128]{2,1,0:T(8,128)(2,1)} async-done(((bf16[768,48,128]{2,1,0:T(8,128)(2,1)}), bf16[96,48,128]{2,1,0:T(8,128)(2,1)}) %reduce-scatter.5.cloned.1.call-update) | async-done | bytes 1179664 | tf_op jit(solution)/shard_map/reduce_scatter | solution.py:54
  907.8 2.7 convert_reduce_fusion
  910.4 1.5 copy.79
  911.9 1.4 broadcast_multiply_fusion
  913.3 1.4 copy.76
  914.7 3.1 fusion.2
  917.8 1.5 copy.80
  919.3 1.4 add_rsqrt_fusion
  920.6 1.4 copy.78
  922.1 4.9 multiply_add_fusion
  (42 shorter events, 0.2 us)
Async XLA Ops:
  6.5 2.7 copy-start
  6.5 4.4 copy-start.17
  6.5 4.4 copy-start.18
  6.5 5.0 copy-start.13
  6.5 130.2 %all-gather.3.cloned.1.call-start = ((), (), s32[]{:S(2)}) async-start(), calls=%async_computation.2 | async-start | bytes 10616832 | tf_op jit(solution)/shard_map/all_gather | solution.py:41
  9.3 1.7 copy-start.5
  10.9 0.6 copy-start.9
  15.3 584.4 %reduce-scatter.3.cloned.1.call-start = ((), (), s32[]{:S(2)}) async-start(), calls=%async_computation.3 | async-start | bytes 40108032 | tf_op jit(solution)/shard_map/reduce_scatter | solution.py:43
  209.8 0.7 copy-start.19
  209.8 0.7 copy-start.20
  209.8 1.3 copy-start.6
  209.8 1.3 copy-start.10
  209.8 1.3 copy-start.15
  209.8 508.0 %all-gather.5.cloned.1.call-start = ((), (), s32[]{:S(2)}) async-start(), calls=%async_computation.4 | async-start | bytes 20054016 | tf_op jit(solution)/shard_map/all_gather | solution.py:52
  599.7 2.7 copy-start.1
  604.1 1.7 copy-start.4
  604.1 1.7 copy-start.23
  608.2 3.8 copy-start.2
  608.2 3.8 copy-start.14
  608.3 3.0 copy-start.7
  611.4 0.6 copy-start.11
  615.7 292.0 %reduce-scatter.5.cloned.1.call-start = ((), (), s32[]{:S(2)}) async-start(), calls=%async_computation.5 | async-start | bytes 10616832 | tf_op jit(solution)/shard_map/reduce_scatter | solution.py:54
  781.7 0.8 copy-start.8
  781.7 0.8 copy-start.12
  781.7 0.9 copy-start.16
  785.7 136.3 %copy-start.21 = (f32[128]{0:T(128)S(1)}, f32[128]{0:T(128)}, u32[]{:S(2)}) copy-start(f32[128]{0:T(128)} %get-tuple-element.11) | copy-start | bytes 1540
  785.7 136.3 %copy-start.22 = (f32[128]{0:T(128)S(1)}, f32[128]{0:T(128)}, u32[]{:S(2)}) copy-start(f32[128]{0:T(128)} %get-tuple-element.22) | copy-start | bytes 1540
  907.8 14.3 %copy-start.3 = (bf16[96,48,128]{2,1,0:T(8,128)(2,1)S(1)}, bf16[96,48,128]{2,1,0:T(8,128)(2,1)}, u32[]{:S(2)}) copy-start(bf16[96,48,128]{2,1,0:T(8,128)(2,1)} %reduce-scatter.5.cloned.1.call-done) | copy-start | bytes 3538948
Sparse Core Ops, SparseCore 0:
  15.4 121.3 all-gather.2
  210.0 389.6 reduce-scatter.2
  615.8 101.9 all-gather.4
  781.9 125.8 reduce-scatter.4
where the time goes:
time: 936 us; the launch traced here: 933 us
  waiting for transfers between devices  727 us (78%)
  local copies, waits for them, and re-layouts  112 us (12%)
  matrix products  55.4 us (6%)
  other arithmetic  25.6 us (3%)
  between operations  13.4 us (1%)
    reduce_scatter x1, waiting for transfers between devices, local(): lax.psum_scatter(jnp.einsum('jkc,ikc->jic', panel_part, left_act, preferr...  385 us
    reduce_scatter x1, waiting for transfers between devices, local(): lax.psum_scatter(jnp.einsum('kic,kjc->ijc', panel_part, right_act, prefer...  122 us
    all_gather x1, waiting for transfers between devices, local(): rows_right = lax.all_gather(right_act, 'row', axis=0, tiled=True)  119 us
    all_gather x1, waiting for transfers between devices, local(): cols_left = lax.all_gather(left_act, 'col', axis=1, tiled=True)  99.9 us
    transpose x1, local copies, waits for them, and re-layouts, local(): jnp.einsum('jkc,ikc->jic', panel_part, left_act, preferred_element_type=j...  37.4 us
    all_gather x1, local copies, waits for them, and re-layouts, local(): cols_left = lax.all_gather(left_act, 'col', axis=1, tiled=True)  32.6 us
    dot_general x1, matrix products, local(): jnp.einsum('jkc,ikc->jic', panel_part, left_act, preferred_element_type=j...  21.7 us
  transfers between devices with their start and end apart: 4, of which 4 were waited for; matrix products, arithmetic and copies ran while one was open for 1% of the time, Pallas kernels for 0%

commit v1 on v0

v1 whole, which is shorter than its diff:
```python
import jax
import jax.numpy as jnp
from jax import lax
from jax.experimental import pallas as pl
from jax.experimental.pallas import tpu as pltpu
from jax.sharding import PartitionSpec as P

epsilon = 1e-05
MESH = pl.DeviceIdType.MESH
DEVICES = 128
F32, BF16 = jnp.float32, jnp.bfloat16
STRIDE = 73


def coordinates():
    row, col = lax.axis_index("row"), lax.axis_index("col")
    return row % 4, col // 4, (row // 4) * 2 + (col // 2) % 2, col % 2


def device_at(x, y, z, core):
    return (z // 2) * 4 + x, y * 4 + (z % 2) * 2 + core


def peer(group, member):
    x, y, z, core = coordinates()
    gx, gy, gz = (x + group) % 2, (y + group // 2) % 2, (z + group // 4) % 2
    mx, my, mz = (x // 2 + member) % 2, (y // 2 + member // 2) % 2, (z // 2 + member // 4) % 2
    core = (core + member // 8) % 2
    channel = (gx + gy * 2 + gz * 4) * 16 + mx + my * 2 + mz * 4 + core * 8
    return device_at(mx * 2 + gx, my * 2 + gy, mz * 2 + gz, core), channel


def sigmoid(values):
    return 0.5 * jnp.tanh(0.5 * values) + 0.5


def norm_columns(values, gain, bias):
    centre = jnp.mean(values, axis=0, keepdims=True)
    shifted = values - centre
    spread = jnp.mean(shifted * shifted, axis=0, keepdims=True)
    return (shifted * lax.rsqrt(spread + epsilon) * gain + bias).astype(BF16)


def turn(blocks):
    lane = lax.broadcasted_iota(jnp.int32, blocks[0].shape, 1)
    first, even = lane < 64, lane % 64 < 32
    a0, a1, a2, a3 = blocks
    b0, b2 = jnp.where(first, a0, pltpu.roll(a2, 64, 1)), jnp.where(first, pltpu.roll(a0, 64, 1), a2)
    b1, b3 = jnp.where(first, a1, pltpu.roll(a3, 64, 1)), jnp.where(first, pltpu.roll(a1, 64, 1), a3)
    c0, c1 = jnp.where(even, b0, pltpu.roll(b1, 32, 1)), jnp.where(even, pltpu.roll(b0, 96, 1), b1)
    c2, c3 = jnp.where(even, b2, pltpu.roll(b3, 32, 1)), jnp.where(even, pltpu.roll(b2, 96, 1), b3)
    return c0, c1, c2, c3


def kernel(
    pair, in_gain, in_bias, mid_gain, mid_bias, w_in, w_gate, w_out, out,
    rows, state, gate, normed, staged, spread_out, outgoing, incoming, sums_out, sums_in,
    left, right, left16, summed, piece, weights, gate_t, out_t, columns,
    copy_sem, own_sem, send_sem, recv_sem,
):
    me_row, me_col = lax.axis_index("row"), lax.axis_index("col")
    me = me_row * 16 + me_col
    barrier = pltpu.get_barrier_semaphore()
    load = pltpu.make_async_copy(pair, rows, copy_sem)
    load.start()

    def greet(step, carry):
        pl.semaphore_signal(barrier, inc=1, device_id=peer(step // 16, step % 16)[0], device_id_type=MESH)
        return carry

    lax.fori_loop(1, DEVICES, greet, 0)

    for u in range(2):
        for part in range(4):
            block = w_in[u, :, part * 128 : (part + 1) * 128].astype(F32).T.astype(BF16)
            for group in range(8):
                weights[u, group, part * 16 : (part + 1) * 16, :] = block[group * 16 : (group + 1) * 16]
        gate_t[u] = w_gate[u].astype(F32).T.astype(BF16)
        out_t[u] = w_out[u].astype(F32).T.astype(BF16)
        for at, row in enumerate((in_gain, in_bias, mid_gain, mid_bias)):
            columns[u, at] = jnp.broadcast_to(row[u : u + 1, :], (128, 128)).T

    load.wait()
    whole_sum = summed.reshape(768, 768)

    def token_rows(tile, quarter):
        start = (tile // 12) * 1536 + tile % 12 + quarter * 12
        return pl.ds(start, 32, stride=48)

    def enter(pair_of, carry):
        halves = []
        for half in range(2):
            tile = pair_of * 2 + half
            tokens = jnp.concatenate([rows[token_rows(tile, q), :] for q in range(4)], axis=0)
            values = tokens.T
            state[tile] = values
            halves.append(norm_columns(values, columns[0, 0], columns[0, 1]))
        normed[pair_of] = jnp.concatenate(halves, axis=1)
        return carry

    lax.fori_loop(0, 18, enter, 0)

    for u in range(2):
        def group_step(group, carry):
            (_, _), first_channel = peer(group, 0)
            which = first_channel // 16

            def project(pair_of, inner):
                projected = jnp.dot(weights[u, which], normed[pair_of], preferred_element_type=F32)
                for side in range(2):
                    at = side * 32
                    acts = sigmoid(projected[at : at + 16]) * projected[at + 16 : at + 32]
                    for octet in range(2):
                        for half in range(2):
                            start = octet * 8 * STRIDE + side * 36 + pair_of * 2 + half
                            staged[pl.ds(start, 8, stride=STRIDE), :] = acts[
                                octet * 8 : octet * 8 + 8, half * 128 : half * 128 + 128
                            ]
                return inner

            lax.fori_loop(0, 18, project, 0)

            def send(member, inner):
                target, channel = peer(group, member)
                outgoing[channel] = staged[pl.ds((channel % 16) * STRIDE, 72), :].astype(BF16)

                @pl.when(group + member > 0)
                def _():
                    pltpu.make_async_remote_copy(
                        src_ref=outgoing.at[channel], dst_ref=incoming.at[me],
                        send_sem=send_sem.at[2 * u], recv_sem=recv_sem.at[2 * u],
                        device_id=target, device_id_type=MESH,
                    ).start()

                @pl.when(group + member == 0)
                def _():
                    pltpu.make_async_copy(outgoing.at[channel], incoming.at[me], own_sem.at[2 * u]).start()

                return inner

            if u == 0:
                @pl.when(group == 0)
                def _():
                    pl.semaphore_wait(barrier, DEVICES - 1)

            lax.fori_loop(0, 16, send, 0)
            return carry

        lax.fori_loop(0, 8, group_step, 0)

        def gates(pair_of, carry):
            value = sigmoid(jnp.dot(gate_t[u], normed[pair_of], preferred_element_type=F32))
            gate[pair_of * 2] = value[:, :128]
            gate[pair_of * 2 + 1] = value[:, 128:]
            return carry

        lax.fori_loop(0, 18, gates, 0)

        others = pl.ds(0, DEVICES - 1)
        pltpu.make_async_copy(outgoing.at[0], incoming.at[0], own_sem.at[2 * u]).wait()
        pltpu.make_async_copy(incoming.at[others], incoming.at[others], recv_sem.at[2 * u]).wait()

        def gather(s, carry):
            for z_hi in range(2):
                turned = turn([incoming[(z_hi * 4 + x) * 16 + s].astype(F32) for x in range(4)])
                for quarter in range(4):
                    for third in range(3):
                        lanes = pl.ds((z_hi * 3 + third) * 128, 128)
                        to = pl.ds(quarter * 12, 12)
                        left[s, to, lanes] = turned[quarter][third * 12 : third * 12 + 12]
                        right[s, to, lanes] = turned[quarter][36 + third * 12 : 48 + third * 12]
            return carry

        lax.fori_loop(0, 16, gather, 0)

        if u == 0:
            left16[...] = left[...].reshape(768, 768).astype(BF16)

            for z_hi in range(2):
                for third in range(3):
                    at = (z_hi * 3 + third) * 128
                    turned = right[:, :, at : at + 128].reshape(768, 128).T.astype(BF16)
                    product = jnp.dot(turned, left16[...], preferred_element_type=F32)
                    for x in range(4):
                        to = (z_hi * 4 + x) * 96 + third * 32
                        whole_sum[to : to + 32, :] = product[x * 32 : x * 32 + 32]
        else:
            flat = left.reshape(768, 768)
            for z_hi in range(2):
                for third in range(3):
                    for x in range(4):
                        at = (z_hi * 4 + x) * 96 + third * 32
                        to = (z_hi * 3 + third) * 128 + x * 32
                        left16[to : to + 32, :] = flat[at : at + 32, :].astype(BF16)
            flat = right.reshape(768, 768)
            for at in range(0, 768, 128):
                whole_sum[at : at + 128, :] = lax.dot_general(
                    flat[at : at + 128, :].astype(BF16), left16[...], (((1,), (1,)), ((), ())),
                    preferred_element_type=F32,
                )

        if u == 1:
            pltpu.make_async_copy(sums_out.at[others], sums_out.at[others], send_sem.at[1]).wait()

        def give_back(step, carry):
            s = (me_col + step * 5) % 16
            for z_hi in range(2):
                for quarter in range(4):
                    for third in range(3):
                        piece[quarter, third * 12 : third * 12 + 12, :] = summed[
                            s, pl.ds(quarter * 12, 12), pl.ds((z_hi * 3 + third) * 128, 128)
                        ]
                turned = turn([piece[quarter] for quarter in range(4)])
                for x in range(4):
                    row = z_hi * 4 + x
                    to = row * 16 + s
                    sums_out[to] = turned[x].astype(BF16)

                    @pl.when(to != me)
                    def _():
                        pltpu.make_async_remote_copy(
                            src_ref=sums_out.at[to], dst_ref=sums_in.at[peer(0, 0)[1]],
                            send_sem=send_sem.at[2 * u + 1], recv_sem=recv_sem.at[2 * u + 1],
                            device_id=(row, s), device_id_type=MESH,
                        ).start()

                    @pl.when(to == me)
                    def _():
                        pltpu.make_async_copy(
                            sums_out.at[to], sums_in.at[peer(0, 0)[1]], own_sem.at[2 * u + 1]
                        ).start()

            return carry

        lax.fori_loop(0, 16, give_back, 0)

        pltpu.make_async_copy(sums_out.at[0], sums_in.at[0], own_sem.at[2 * u + 1]).wait()
        pltpu.make_async_copy(sums_in.at[others], sums_in.at[others], recv_sem.at[2 * u + 1]).wait()
        pltpu.make_async_copy(outgoing.at[others], outgoing.at[others], send_sem.at[2 * u]).wait()

        def widen(channel, carry):
            spread_out[channel, 0:36, :] = sums_in[channel].astype(F32)
            return carry

        lax.fori_loop(0, DEVICES, widen, 0)
        flat_sums = spread_out.reshape(128 * 40, 128)

        def finish(pair_of, carry):
            mixed = []
            for half in range(2):
                values = flat_sums[pl.ds(pair_of * 2 + half, 128, stride=40), :]
                mixed.append(norm_columns(values, columns[u, 2], columns[u, 3]))
            update = jnp.dot(out_t[u], jnp.concatenate(mixed, axis=1), preferred_element_type=F32)
            halves = []
            for half in range(2):
                tile = pair_of * 2 + half
                values = state[tile] + gate[tile] * update[:, half * 128 : half * 128 + 128]
                if u == 0:
                    state[tile] = values
                    halves.append(norm_columns(values, columns[1, 0], columns[1, 1]))
                else:
                    tokens = values.T
                    for q in range(4):
                        rows[token_rows(tile, q), :] = tokens[q * 32 : q * 32 + 32]
            if u == 0:
                normed[pair_of] = jnp.concatenate(halves, axis=1)
            return carry

        lax.fori_loop(0, 18, finish, 0)

    pltpu.make_async_copy(sums_out.at[others], sums_out.at[others], send_sem.at[3]).wait()
    store = pltpu.make_async_copy(rows, out, copy_sem)
    store.start()
    store.wait()


def local(pair, *parameters):
    vmem, anywhere = pl.BlockSpec(memory_space=pltpu.VMEM), pl.BlockSpec(memory_space=pl.ANY)
    done = pl.pallas_call(
        kernel,
        out_shape=jax.ShapeDtypeStruct((4608, 128), F32),
        in_specs=[anywhere] + [vmem] * 7,
        out_specs=anywhere,
        scratch_shapes=[
            pltpu.VMEM((4608, 128), F32),
            pltpu.VMEM((36, 128, 128), F32),
            pltpu.VMEM((36, 128, 128), F32),
            pltpu.VMEM((18, 128, 256), BF16),
            pltpu.VMEM((16 * STRIDE + 8, 128), F32),
            pltpu.VMEM((128, 40, 128), F32),
            pltpu.VMEM((128, 72, 128), BF16),
            pltpu.VMEM((128, 72, 128), BF16),
            pltpu.VMEM((128, 36, 128), BF16),
            pltpu.VMEM((128, 36, 128), BF16),
            pltpu.VMEM((16, 48, 768), F32),
            pltpu.VMEM((16, 48, 768), F32),
            pltpu.VMEM((768, 768), BF16),
            pltpu.VMEM((16, 48, 768), F32),
            pltpu.VMEM((4, 36, 128), F32),
            pltpu.VMEM((2, 8, 64, 128), BF16),
            pltpu.VMEM((2, 128, 128), BF16),
            pltpu.VMEM((2, 128, 128), BF16),
            pltpu.VMEM((2, 4, 128, 128), F32),
            pltpu.SemaphoreType.DMA,
            pltpu.SemaphoreType.DMA((4,)),
            pltpu.SemaphoreType.DMA((4,)),
            pltpu.SemaphoreType.DMA((4,)),
        ],
        compiler_params=pltpu.CompilerParams(
            collective_id=0, has_side_effects=True, vmem_limit_bytes=56 * 2**20
        ),
    )(pair.reshape(4608, 128), *parameters)
    return done.reshape(96, 48, 128)


def solution(mesh):
    return jax.shard_map(
        local,
        mesh=mesh,
        in_specs=(P("row", "col", None), P(), P(), P(), P(), P(), P(), P()),
        out_specs=P("row", "col", None),
        check_vma=False,
    )
```

time: 936 us -> 154 us (0.16)
  waiting for transfers between devices: 727 us -> 0 us
  Pallas kernels: 0 us -> 150 us
  local copies, waits for them, and re-layouts: 112 us -> 3.22 us
  matrix products: 55.4 us -> 0 us
  other arithmetic: 25.6 us -> 0 us
  between operations: 13.4 us -> 0.01 us
    reduce_scatter x2 -> x0, waiting for transfers between devices: 508 us -> none  [the longest x1 385 us: local(): lax.psum_scatter(jnp.einsum('jkc,ikc->jic', panel_part, left_act, preferr...]
    all_gather x2 -> x0, waiting for transfers between devices: 219 us -> none  [the longest x1 119 us: local(): rows_right = lax.all_gather(right_act, 'row', axis=0, tiled=True)]
    pallas_call x0 -> x1, Pallas kernels: none -> 150 us  [local(): pl.pallas_call(kernel, out_shape=jax.ShapeDtypeStruct((4608, 128), F32),...]
    dot_general x8 -> x0, matrix products: 55.4 us -> none  [the longest x1 21.7 us: local(): jnp.einsum('jkc,ikc->jic', panel_part, left_act, preferred_element_type=j...]
    all_gather x2 -> x0, local copies, waits for them, and re-layouts: 46.6 us -> none  [the longest x1 32.6 us: local(): cols_left = lax.all_gather(left_act, 'col', axis=1, tiled=True)]
    transpose x1 -> x0, local copies, waits for them, and re-layouts: 37.4 us -> none  [local(): jnp.einsum('jkc,ikc->jic', panel_part, left_act, preferred_element_type=j...]
    convert_element_type x3 -> x0, local copies, waits for them, and re-layouts: 18 us -> none  [the longest x1 14 us: local(): tri_sum = lax.psum_scatter(jnp.einsum('kic,kjc->ijc', panel_part, right_a...]
    reduce_sum x7 -> x0, other arithmetic: 16.9 us -> none  [the longest x4 9 us: layer_norm(): spread = jnp.mean(shifted * shifted, axis=-1, keepdims=True)]
  transfers between devices with their start and end apart: 4 -> 0, of which waited for: 4 -> 0; matrix products, arithmetic and copies ran while one was open for 1% -> 0% of each run, Pallas kernels for 0% -> 0%
where the time goes in v1:
time: 154 us
  Pallas kernels  150 us (97%)
  local copies, waits for them, and re-layouts  3.22 us (2%)
    pallas_call x1, Pallas kernels, local(): pl.pallas_call(kernel, out_shape=jax.ShapeDtypeStruct((4608, 128), F32),...  150 us
    unnamed x1, local copies, waits for them, and re-layouts  3.22 us

profile of v1, /device:TPU:1, one launch (start us, length us, event | category | flops | bytes accessed | tf_op | source)
XLA Modules:
  0.0 153.5 jit_solution(11858360510035786444)
XLA Ops:
  0.0 150.3 %shard_map.82 = f32[4608,128]{1,0:T(8,128)} custom-call(f32[4608,128]{1,0:T(8,128)} %bitcast.3, f32[2,128]{1,0:T(2,128)} %in_gain.1, f32[2,128]{1,0:T(2,128)} %in_bias.1, f32[2,128]{1,0:T(2,128)} %mid_gain.1, f32[2,128]{1,0:T(2,128)} %mid_bias.1, bf16[2,128,512]{2,1,0:T(8,128)(2,1)} %w_in.1, bf16[2,128,128]{2,1,0:T(8,128)(2,1)} %w_gate.1, ...), custom_call_target="tpu_custom_call" | custom-call | tf_op jit(solution)/shard_map/pallas_call | solution.py:279
  150.3 3.2 %copy.10 = f32[96,48,128]{2,1,0:T(8,128)} copy(f32[96,48,128]{2,1,0:T(8,128)} %bitcast.2) | data formatting | bytes 4718592

commit v2 on v1

v2 whole, which is shorter than its diff:
```python
import jax
import jax.numpy as jnp
from jax import lax
from jax.experimental import pallas as pl
from jax.experimental.pallas import tpu as pltpu
from jax.sharding import PartitionSpec as P

epsilon = 1e-05
MESH = pl.DeviceIdType.MESH
DEVICES = 128
F32, BF16 = jnp.float32, jnp.bfloat16
STRIDE = 73
WIDE = 41


def add_mod(value, offset, size):
    return lax.rem(value + offset, size)


def device_at(x, y, z, core):
    return lax.div(z, 2) * 4 + x, y * 4 + lax.rem(z, 2) * 2 + core


def sigmoid(values):
    return 0.5 * jnp.tanh(0.5 * values) + 0.5


def norm_columns(values, gain, bias):
    centre = jnp.mean(values, axis=0, keepdims=True)
    shifted = values - centre
    spread = jnp.mean(shifted * shifted, axis=0, keepdims=True)
    return (shifted * lax.rsqrt(spread + epsilon) * gain + bias).astype(BF16)


def turn(blocks):
    lane = lax.broadcasted_iota(jnp.int32, blocks[0].shape, 1)
    first, even = lane < 64, lane % 64 < 32
    a0, a1, a2, a3 = blocks
    b0, b2 = jnp.where(first, a0, pltpu.roll(a2, 64, 1)), jnp.where(first, pltpu.roll(a0, 64, 1), a2)
    b1, b3 = jnp.where(first, a1, pltpu.roll(a3, 64, 1)), jnp.where(first, pltpu.roll(a1, 64, 1), a3)
    c0, c1 = jnp.where(even, b0, pltpu.roll(b1, 32, 1)), jnp.where(even, pltpu.roll(b0, 96, 1), b1)
    c2, c3 = jnp.where(even, b2, pltpu.roll(b3, 32, 1)), jnp.where(even, pltpu.roll(b2, 96, 1), b3)
    return c0, c1, c2, c3


def kernel(
    pair, in_gain_h, in_bias_h, mid_gain_h, mid_bias_h, w_in_h, w_gate_h, w_out_h, out,
    in_gain, in_bias, mid_gain, mid_bias, w_in, w_gate, w_out,
    rows, state, gate, normed, staged, widened, outgoing, incoming, sums_out, sums_in,
    slab_left, slab_right, left16, right16, right_t, summed, piece, weights, gate_t, out_t, columns,
    copy_sem, param_sem, own_sem, send_sem, recv_sem, sums_sem, plane_sem,
):
    row, col = lax.axis_index("row"), lax.axis_index("col")
    me = row * 16 + col
    x, z_hi = lax.rem(row, 4), lax.div(row, 4)
    y, z_lo, core = lax.div(col, 4), lax.rem(lax.div(col, 2), 2), lax.rem(col, 2)
    z = z_hi * 2 + z_lo
    y_lo, y_hi = lax.rem(y, 2), lax.div(y, 2)
    my_channel = (y_lo + z_lo * 2 + core * 4) * 16 + x + y_hi * 4 + z_hi * 8

    loads = [
        pltpu.make_async_copy(pair.at[pl.ds(i * 1536, 1536)], rows.at[pl.ds(i * 1536, 1536)], copy_sem.at[i])
        for i in range(3)
    ]
    parameters = [
        pltpu.make_async_copy(from_hbm, to, param_sem.at[i])
        for i, (from_hbm, to) in enumerate(
            (
                (in_gain_h, in_gain), (in_bias_h, in_bias), (w_in_h, w_in), (mid_gain_h, mid_gain),
                (mid_bias_h, mid_bias), (w_gate_h, w_gate), (w_out_h, w_out),
            )
        )
    ]
    for load in parameters[:3] + loads + parameters[3:]:
        load.start()

    along_x = [device_at(add_mod(x, i, 4), y, z, core) for i in range(1, 4)]
    along_y = [device_at(x, add_mod(y, i, 4), z, core) for i in range(1, 4)]
    along_z = [device_at(x, y, add_mod(z, i, 4), core) for i in range(1, 4)]
    other_core = [device_at(x, y, z, 1 - core)]
    barrier = pltpu.get_barrier_semaphore()

    def tell(semaphore, devices):
        for device in devices:
            pl.semaphore_signal(semaphore, inc=1, device_id=device, device_id_type=MESH)

    tell(barrier, along_x + along_y + along_z + other_core)

    def prepare(u, what):
        if what == "in":
            for at, source in enumerate((in_gain, in_bias)):
                columns[u, at] = jnp.broadcast_to(source[u : u + 1, :], (128, 128)).T
            for part in range(4):
                block = w_in[u, :, part * 128 : (part + 1) * 128].astype(F32).T.astype(BF16)
                for group in range(8):
                    weights[u, group, part * 16 : (part + 1) * 16, :] = block[group * 16 : (group + 1) * 16]
        else:
            gate_t[u] = w_gate[u].astype(F32).T.astype(BF16)
            out_t[u] = w_out[u].astype(F32).T.astype(BF16)
            for at, source in enumerate((mid_gain, mid_bias)):
                columns[u, 2 + at] = jnp.broadcast_to(source[u : u + 1, :], (128, 128)).T

    for load in parameters[:3]:
        load.wait()
    prepare(0, "in")

    def token_rows(tile, quarter):
        start = lax.div(tile, 12) * 1536 + lax.rem(tile, 12) + quarter * 12
        return pl.ds(start, 32, stride=48)

    def enter(pair_of, carry):
        halves = []
        for half in range(2):
            tile = pair_of * 2 + half
            tokens = jnp.concatenate([rows[token_rows(tile, q), :] for q in range(4)], axis=0)
            values = tokens.T
            state[tile] = values
            halves.append(norm_columns(values, columns[0, 0], columns[0, 1]))
        normed[pair_of] = jnp.concatenate(halves, axis=1)
        return carry

    loads[0].wait()
    pl.semaphore_wait(barrier, 10)
    tell(plane_sem.at[0], along_y)
    lax.fori_loop(0, 6, enter, 0, unroll=2)
    loads[1].wait()
    pl.semaphore_wait(plane_sem.at[0], 3)
    tell(plane_sem.at[1], along_z)
    lax.fori_loop(6, 12, enter, 0, unroll=2)
    loads[2].wait()
    pl.semaphore_wait(plane_sem.at[1], 3)
    tell(plane_sem.at[2], other_core)
    lax.fori_loop(12, 18, enter, 0, unroll=2)

    others = pl.ds(0, DEVICES - 1)
    slab_left[96:128, :] = jnp.zeros((32, 768), F32)
    slab_right[96:128, :] = jnp.zeros((32, 768), F32)

    for u in range(2):
        def group_step(group, carry):
            to_y, to_z = add_mod(y_lo, group, 2), add_mod(z_lo, lax.div(group, 2), 2)
            to_core = add_mod(core, lax.div(group, 4), 2)
            which = to_y + to_z * 2 + to_core * 4

            def project(pair_of, inner):
                projected = jnp.dot(weights[u, which], normed[pair_of], preferred_element_type=F32)
                for side in range(2):
                    at = side * 32
                    acts = sigmoid(projected[at : at + 16]) * projected[at + 16 : at + 32]
                    for octet in range(2):
                        for half in range(2):
                            start = octet * 8 * STRIDE + side * 36 + pair_of * 2 + half
                            staged[pl.ds(start, 8, stride=STRIDE), :] = acts[
                                octet * 8 : octet * 8 + 8, half * 128 : half * 128 + 128
                            ]
                return inner

            lax.fori_loop(0, 18, project, 0, unroll=6)

            if u == 0:
                @pl.when(group == 0)
                def _():
                    pl.semaphore_wait(plane_sem.at[2], 1)

            def send(member, inner):
                at_x = add_mod(x, member, 4)
                at_y, at_z = add_mod(y_hi, lax.div(member, 4), 2), add_mod(z_hi, lax.div(member, 8), 2)
                place = at_x + at_y * 4 + at_z * 8
                channel = which * 16 + place
                outgoing[channel] = staged[pl.ds(place * STRIDE, 72), :].astype(BF16)

                @pl.when(group + member > 0)
                def _():
                    pltpu.make_async_remote_copy(
                        src_ref=outgoing.at[channel], dst_ref=incoming.at[me],
                        send_sem=send_sem.at[2 * u], recv_sem=recv_sem.at[u * 8 + group],
                        device_id=(at_z * 4 + at_x, at_y * 8 + to_y * 4 + to_z * 2 + to_core),
                        device_id_type=MESH,
                    ).start()

                @pl.when(group + member == 0)
                def _():
                    pltpu.make_async_copy(outgoing.at[channel], incoming.at[me], own_sem.at[2 * u]).start()

                return inner

            lax.fori_loop(0, 16, send, 0, unroll=4)
            return carry

        lax.fori_loop(0, 8, group_step, 0)

        if u == 0:
            for load in parameters[3:]:
                load.wait()
            prepare(0, "out")
            prepare(1, "in")
            prepare(1, "out")

        def gates(pair_of, carry):
            value = sigmoid(jnp.dot(gate_t[u], normed[pair_of], preferred_element_type=F32))
            gate[pair_of * 2] = value[:, :128]
            gate[pair_of * 2 + 1] = value[:, 128:]
            return carry

        lax.fori_loop(0, 18, gates, 0, unroll=2)

        pltpu.make_async_copy(outgoing.at[0], incoming.at[0], own_sem.at[2 * u]).wait()

        def gather(group, carry):
            @pl.when(group == 0)
            def _():
                part = incoming.at[pl.ds(0, 15)]
                pltpu.make_async_copy(part, part, recv_sem.at[u * 8]).wait()

            @pl.when(group > 0)
            def _():
                part = incoming.at[pl.ds(0, 16)]
                pltpu.make_async_copy(part, part, recv_sem.at[u * 8 + group]).wait()

            from_y, from_z = add_mod(y_lo, group, 2), add_mod(z_lo, lax.div(group, 2), 2)
            from_core = add_mod(core, lax.div(group, 4), 2)
            column = from_y * 4 + from_z * 2 + from_core
            for h in range(2):
                for hi in range(2):
                    turned = turn(
                        [incoming[(hi * 4 + at) * 16 + h * 8 + column].astype(F32) for at in range(4)]
                    )
                    for quarter in range(4):
                        for third in range(3):
                            lanes = pl.ds((hi * 3 + third) * 128, 128)
                            to = pl.ds(h * 48 + quarter * 12, 12)
                            slab_left[to, lanes] = turned[quarter][third * 12 : third * 12 + 12]
                            slab_right[to, lanes] = turned[quarter][36 + third * 12 : 48 + third * 12]
            if u == 0:
                left16[group] = slab_left[...].astype(BF16)
                for hi in range(2):
                    for third in range(3):
                        lanes = pl.ds((hi * 3 + third) * 128, 128)
                        flipped = slab_right[:, lanes].T.astype(BF16)
                        for at in range(4):
                            right_t[
                                pl.ds((hi * 4 + at) * 96 + third * 32, 32),
                                pl.ds(pl.multiple_of(group * 128, 128), 128),
                            ] = flipped[at * 32 : at * 32 + 32]
            else:
                for h in range(2):
                    right16[h * 8 + column] = slab_right[h * 48 : h * 48 + 48, :].astype(BF16)
                    for part in range(3):
                        sixth = from_core * 3 + part
                        to = h * 384 + lax.div(sixth, 2) * 128 + (from_y * 2 + from_z) * 32 + lax.rem(sixth, 2) * 16
                        at = h * 48 + part * 16
                        left16.reshape(1024, 768)[pl.ds(pl.multiple_of(to, 16), 16), :] = slab_left[
                            at : at + 16, :
                        ].astype(BF16)
            return carry

        lax.fori_loop(0, 8, gather, 0)

        if u == 1:
            pltpu.make_async_copy(sums_out.at[others], sums_out.at[others], send_sem.at[1]).wait()

        def give_back(step, carry):
            turn_y = lax.div(step, 2)
            to_y = add_mod(y, turn_y + lax.div(turn_y, 2) * (5 - 2 * turn_y), 4)
            to_z = add_mod(z_lo, step, 2)
            pair_at = to_y * 2 + to_z
            rows_at = pl.ds(pl.multiple_of(pair_at * 96, 96), 96)
            if u == 0:
                product = jnp.dot(right_t[rows_at, :], left16.reshape(1024, 768)[...], preferred_element_type=F32)
            else:
                product = lax.dot_general(
                    right16.reshape(768, 768)[rows_at, :], left16.reshape(1024, 768)[0:768, :],
                    (((1,), (1,)), ((), ())), preferred_element_type=F32,
                )
            summed[...] = product
            for to_core in range(2):
                s = pair_at * 2 + to_core
                for hi in range(2):
                    for quarter in range(4):
                        for third in range(3):
                            piece[quarter, third * 12 : third * 12 + 12, :] = summed[
                                pl.ds(to_core * 48 + quarter * 12, 12), pl.ds((hi * 3 + third) * 128, 128)
                            ]
                    turned = turn([piece[quarter] for quarter in range(4)])
                    for at in range(4):
                        to_row = hi * 4 + at
                        to = to_row * 16 + s
                        sums_out[to] = turned[at].astype(BF16)

                        @pl.when(to != me)
                        def _():
                            pltpu.make_async_remote_copy(
                                src_ref=sums_out.at[to], dst_ref=sums_in.at[my_channel],
                                send_sem=send_sem.at[2 * u + 1], recv_sem=sums_sem.at[u],
                                device_id=(to_row, s), device_id_type=MESH,
                            ).start()

                        @pl.when(to == me)
                        def _():
                            pltpu.make_async_copy(
                                sums_out.at[to], sums_in.at[my_channel], own_sem.at[2 * u + 1]
                            ).start()

            return carry

        lax.fori_loop(0, 8, give_back, 0)

        pltpu.make_async_copy(sums_out.at[0], sums_in.at[0], own_sem.at[2 * u + 1]).wait()
        pltpu.make_async_copy(sums_in.at[others], sums_in.at[others], sums_sem.at[u]).wait()
        pltpu.make_async_copy(outgoing.at[others], outgoing.at[others], send_sem.at[2 * u]).wait()

        def widen(channel, carry):
            widened[pl.ds(channel * WIDE, 36), :] = sums_in[channel].astype(F32)
            return carry

        lax.fori_loop(0, DEVICES, widen, 0, unroll=8)

        def finish(pair_of, carry):
            mixed = []
            for half in range(2):
                values = widened[pl.ds(pair_of * 2 + half, 128, stride=WIDE), :]
                mixed.append(norm_columns(values, columns[u, 2], columns[u, 3]))
            update = jnp.dot(out_t[u], jnp.concatenate(mixed, axis=1), preferred_element_type=F32)
            halves = []
            for half in range(2):
                tile = pair_of * 2 + half
                values = state[tile] + gate[tile] * update[:, half * 128 : half * 128 + 128]
                if u == 0:
                    state[tile] = values
                    halves.append(norm_columns(values, columns[1, 0], columns[1, 1]))
                else:
                    tokens = values.T
                    for q in range(4):
                        rows[token_rows(tile, q), :] = tokens[q * 32 : q * 32 + 32]
            if u == 0:
                normed[pair_of] = jnp.concatenate(halves, axis=1)
            return carry

        if u == 0:
            lax.fori_loop(0, 18, finish, 0, unroll=2)
        else:
            stores = []
            for i in range(3):
                lax.fori_loop(i * 6, i * 6 + 6, finish, 0, unroll=2)
                stores.append(
                    pltpu.make_async_copy(
                        rows.at[pl.ds(i * 1536, 1536)], out.at[pl.ds(i * 1536, 1536)], copy_sem.at[i]
                    )
                )
                stores[-1].start()

    pltpu.make_async_copy(sums_out.at[others], sums_out.at[others], send_sem.at[3]).wait()
    for store in stores:
        store.wait()


def local(pair, *parameters):
    anywhere = pl.BlockSpec(memory_space=pl.ANY)
    done = pl.pallas_call(
        kernel,
        out_shape=jax.ShapeDtypeStruct((4608, 128), F32),
        in_specs=[anywhere] * 8,
        out_specs=anywhere,
        scratch_shapes=[pltpu.VMEM(p.shape, p.dtype) for p in parameters] + [
            pltpu.VMEM((4608, 128), F32),
            pltpu.VMEM((36, 128, 128), F32),
            pltpu.VMEM((36, 128, 128), F32),
            pltpu.VMEM((18, 128, 256), BF16),
            pltpu.VMEM((16 * STRIDE + 8, 128), F32),
            pltpu.VMEM((128 * WIDE, 128), F32),
            pltpu.VMEM((128, 72, 128), BF16),
            pltpu.VMEM((128, 72, 128), BF16),
            pltpu.VMEM((128, 36, 128), BF16),
            pltpu.VMEM((128, 36, 128), BF16),
            pltpu.VMEM((128, 768), F32),
            pltpu.VMEM((128, 768), F32),
            pltpu.VMEM((8, 128, 768), BF16),
            pltpu.VMEM((16, 48, 768), BF16),
            pltpu.VMEM((768, 1024), BF16),
            pltpu.VMEM((96, 768), F32),
            pltpu.VMEM((4, 36, 128), F32),
            pltpu.VMEM((2, 8, 64, 128), BF16),
            pltpu.VMEM((2, 128, 128), BF16),
            pltpu.VMEM((2, 128, 128), BF16),
            pltpu.VMEM((2, 4, 128, 128), F32),
            pltpu.SemaphoreType.DMA((3,)),
            pltpu.SemaphoreType.DMA((7,)),
            pltpu.SemaphoreType.DMA((4,)),
            pltpu.SemaphoreType.DMA((4,)),
            pltpu.SemaphoreType.DMA((16,)),
            pltpu.SemaphoreType.DMA((2,)),
            pltpu.SemaphoreType.REGULAR((3,)),
        ],
        compiler_params=pltpu.CompilerParams(
            collective_id=0, has_side_effects=True, vmem_limit_bytes=56 * 2**20
        ),
    )(pair.reshape(4608, 128), *parameters)
    return done.reshape(96, 48, 128)


def solution(mesh):
    return jax.shard_map(
        local,
        mesh=mesh,
        in_specs=(P("row", "col", None), P(), P(), P(), P(), P(), P(), P()),
        out_specs=P("row", "col", None),
        check_vma=False,
    )
```

time: 154 us -> 129 us (0.84)
  Pallas kernels: 150 us -> 125 us
    pallas_call x1, Pallas kernels: 150 us -> 125 us  [local(): pl.pallas_call(kernel, out_shape=jax.ShapeDtypeStruct((4608, 128), F32),...]
where the time goes in v2:
time: 129 us; the launch traced here: 128 us
  Pallas kernels  125 us (97%)
  local copies, waits for them, and re-layouts  3.22 us (2%)
    pallas_call x1, Pallas kernels, local(): pl.pallas_call(kernel, out_shape=jax.ShapeDtypeStruct((4608, 128), F32),...  125 us
    unnamed x1, local copies, waits for them, and re-layouts  3.22 us

profile of v2, /device:TPU:1, one launch (start us, length us, event | category | flops | bytes accessed | tf_op | source)
XLA Modules:
  0.0 128.5 jit_solution(16653031790316718518)
XLA Ops:
  0.0 125.2 %shard_map.82 = f32[4608,128]{1,0:T(8,128)} custom-call(f32[4608,128]{1,0:T(8,128)} %bitcast.3, f32[2,128]{1,0:T(2,128)} %in_gain_h.1, f32[2,128]{1,0:T(2,128)} %in_bias_h.1, f32[2,128]{1,0:T(2,128)} %mid_gain_h.1, f32[2,128]{1,0:T(2,128)} %mid_bias_h.1, bf16[2,128,512]{2,1,0:T(8,128)(2,1)} %w_in_h.1, bf16[2,128,128]{2,1,0:T(8,128)(2,1)} %w_gate_h.1, ...), custom_call_target="tpu_custom_call" | custom-call | tf_op jit(solution)/shard_map/pallas_call | solution.py:359
  125.2 3.2 %copy.10 = f32[96,48,128]{2,1,0:T(8,128)} copy(f32[96,48,128]{2,1,0:T(8,128)} %bitcast.2) | data formatting | bytes 4718592

commit v3 on v2

v3 whole, which is shorter than its diff:
```python
import jax
import jax.numpy as jnp
from jax import lax
from jax.experimental import pallas as pl
from jax.experimental.pallas import tpu as pltpu
from jax.sharding import PartitionSpec as P

epsilon = 1e-05
MESH = pl.DeviceIdType.MESH
DEVICES = 128
F32, BF16 = jnp.float32, jnp.bfloat16
STRIDE = 41
WIDE = 41
FIRST_ROW, ROWS = (0, 16), (16, 20)
SEGMENTS = (((0, 0, 0, 12), (12, 1, 0, 4)), ((0, 1, 4, 8), (8, 2, 0, 12)))


def add_mod(value, offset, size):
    return lax.rem(value + offset, size)


def device_at(x, y, z, core):
    return lax.div(z, 2) * 4 + x, y * 4 + lax.rem(z, 2) * 2 + core


def sigmoid(values):
    return 0.5 * jnp.tanh(0.5 * values) + 0.5


def norm_columns(values, gain, bias):
    centre = jnp.mean(values, axis=0, keepdims=True)
    shifted = values - centre
    spread = jnp.mean(shifted * shifted, axis=0, keepdims=True)
    return (shifted * lax.rsqrt(spread + epsilon) * gain + bias).astype(BF16)


def turn(blocks):
    lane = lax.broadcasted_iota(jnp.int32, blocks[0].shape, 1)
    first, even = lane < 64, lane % 64 < 32
    a0, a1, a2, a3 = blocks
    b0, b2 = jnp.where(first, a0, pltpu.roll(a2, 64, 1)), jnp.where(first, pltpu.roll(a0, 64, 1), a2)
    b1, b3 = jnp.where(first, a1, pltpu.roll(a3, 64, 1)), jnp.where(first, pltpu.roll(a1, 64, 1), a3)
    c0, c1 = jnp.where(even, b0, pltpu.roll(b1, 32, 1)), jnp.where(even, pltpu.roll(b0, 96, 1), b1)
    c2, c3 = jnp.where(even, b2, pltpu.roll(b3, 32, 1)), jnp.where(even, pltpu.roll(b2, 96, 1), b3)
    return c0, c1, c2, c3


def kernel(
    pair, in_gain_h, in_bias_h, mid_gain_h, mid_bias_h, w_in_h, w_gate_h, w_out_h, out,
    in_gain, in_bias, mid_gain, mid_bias, w_in, w_gate, w_out,
    rows, state, gate, normed, staged, widened, outgoing0, outgoing1, incoming0, incoming1,
    sums_out0, sums_out1, sums_in0, sums_in1,
    slab_left, slab_right, left16, right16, right_t, summed0, summed1, piece, weights, gate_t, out_t, columns,
    copy_sem, param_sem, own_sem, own_sums_sem, send_sem, sums_send_sem, recv_sem, sums_sem, plane_sem,
):
    row, col = lax.axis_index("row"), lax.axis_index("col")
    me = row * 16 + col
    x, z_hi = lax.rem(row, 4), lax.div(row, 4)
    y, z_lo, core = lax.div(col, 4), lax.rem(lax.div(col, 2), 2), lax.rem(col, 2)
    z = z_hi * 2 + z_lo
    y_lo, y_hi = lax.rem(y, 2), lax.div(y, 2)
    my_channel = (y_lo + z_lo * 2 + core * 4) * 16 + x + y_hi * 4 + z_hi * 8

    loads = [
        pltpu.make_async_copy(pair.at[pl.ds(i * 1536, 1536)], rows.at[pl.ds(i * 1536, 1536)], copy_sem.at[i])
        for i in range(3)
    ]
    parameters = [
        pltpu.make_async_copy(from_hbm, to, param_sem.at[i])
        for i, (from_hbm, to) in enumerate(
            (
                (in_gain_h, in_gain), (in_bias_h, in_bias), (w_in_h, w_in), (mid_gain_h, mid_gain),
                (mid_bias_h, mid_bias), (w_gate_h, w_gate), (w_out_h, w_out),
            )
        )
    ]
    for load in parameters[:3] + loads + parameters[3:]:
        load.start()

    outgoing, incoming = (outgoing0, outgoing1), (incoming0, incoming1)
    sums_out, sums_in = (sums_out0, sums_out1), (sums_in0, sums_in1)

    plane = [
        device_at(add_mod(x, i, 4), add_mod(y, j, 4), z, core) for i in range(4) for j in range(4) if i + j
    ]
    line = [
        device_at(x, y, add_mod(z, i, 4), add_mod(core, j, 2)) for i in range(4) for j in range(2) if i + j
    ]
    barrier = pltpu.get_barrier_semaphore()

    def tell(semaphore, devices):
        for device in devices:
            pl.semaphore_signal(semaphore, inc=1, device_id=device, device_id_type=MESH)

    tell(barrier, plane + line)

    def prepare(u, what):
        if what == "in":
            for at, source in enumerate((in_gain, in_bias)):
                columns[u, at] = jnp.broadcast_to(source[u : u + 1, :], (128, 128)).T
            for part in range(4):
                block = w_in[u, :, part * 128 : (part + 1) * 128].astype(F32).T.astype(BF16)
                for group in range(8):
                    weights[u, group, part * 16 : (part + 1) * 16, :] = block[group * 16 : (group + 1) * 16]
        else:
            gate_t[u] = w_gate[u].astype(F32).T.astype(BF16)
            out_t[u] = w_out[u].astype(F32).T.astype(BF16)
            for at, source in enumerate((mid_gain, mid_bias)):
                columns[u, 2 + at] = jnp.broadcast_to(source[u : u + 1, :], (128, 128)).T

    for load in parameters[:3]:
        load.wait()
    prepare(0, "in")

    def token_rows(tile, quarter):
        start = lax.div(tile, 12) * 1536 + lax.rem(tile, 12) + quarter * 12
        return pl.ds(start, 32, stride=48)

    def enter(pair_of, carry):
        halves = []
        for half in range(2):
            tile = pair_of * 2 + half
            tokens = jnp.concatenate([rows[token_rows(tile, q), :] for q in range(4)], axis=0)
            values = tokens.T
            state[tile] = values
            halves.append(norm_columns(values, columns[0, 0], columns[0, 1]))
        normed[pair_of] = jnp.concatenate(halves, axis=1)
        return carry

    loads[0].wait()
    lax.fori_loop(0, 6, enter, 0, unroll=2)
    pl.semaphore_wait(barrier, len(plane) + len(line))
    tell(plane_sem, line)
    loads[1].wait()
    lax.fori_loop(6, 8, enter, 0, unroll=2)

    others = pl.ds(0, DEVICES - 1)
    slab_left[96:128, :] = jnp.zeros((32, 768), F32)
    slab_right[96:128, :] = jnp.zeros((32, 768), F32)

    def project_and_send(u, part):
        base, count = FIRST_ROW[part], ROWS[part]

        def group_step(group, carry):
            to_y, to_z = add_mod(y_lo, group, 2), add_mod(z_lo, lax.div(group, 2), 2)
            to_core = add_mod(core, lax.div(group, 4), 2)
            which = to_y + to_z * 2 + to_core * 4

            def project(pair_of, inner):
                projected = jnp.dot(weights[u, which], normed[pair_of], preferred_element_type=F32)
                for side in range(2):
                    at = side * 32
                    acts = sigmoid(projected[at : at + 16]) * projected[at + 16 : at + 32]
                    for octet in range(2):
                        for half in range(2):
                            start = octet * 8 * STRIDE + side * count + pair_of * 2 + half - base
                            staged[pl.ds(start, 8, stride=STRIDE), :] = acts[
                                octet * 8 : octet * 8 + 8, half * 128 : half * 128 + 128
                            ]
                return inner

            lax.fori_loop(base // 2, (base + count) // 2, project, 0, unroll=count // 4)

            if u == 0 and part == 0:
                @pl.when(group == 0)
                def _():
                    pl.semaphore_wait(plane_sem, len(line))

            def send(member, inner):
                along = lax.rem(lax.div(member, 4) + lax.rem(member, 4) + 1, 4)
                at_x = add_mod(x, along + core * (4 - 2 * along), 4)
                at_y, at_z = add_mod(y_hi, member, 2), add_mod(z_hi, lax.div(member, 2), 2)
                place = at_x + at_y * 4 + at_z * 8
                channel = which * 16 + place
                outgoing[part][channel] = staged[pl.ds(place * STRIDE, 2 * count), :].astype(BF16)

                @pl.when(channel != my_channel)
                def _():
                    pltpu.make_async_remote_copy(
                        src_ref=outgoing[part].at[channel], dst_ref=incoming[part].at[me],
                        send_sem=send_sem.at[2 * u + part],
                        recv_sem=recv_sem.at[(2 * u + part) * 8 + group],
                        device_id=(at_z * 4 + at_x, at_y * 8 + to_y * 4 + to_z * 2 + to_core),
                        device_id_type=MESH,
                    ).start()

                @pl.when(channel == my_channel)
                def _():
                    pltpu.make_async_copy(
                        outgoing[part].at[channel], incoming[part].at[me], own_sem.at[2 * u + part]
                    ).start()

                return inner

            lax.fori_loop(0, 16, send, 0, unroll=4)
            return carry

        lax.fori_loop(0, 8, group_step, 0)

    project_and_send(0, 0)
    loads[2].wait()
    lax.fori_loop(8, 18, enter, 0, unroll=2)
    project_and_send(0, 1)

    for u in range(2):
        if u == 0:
            for load in parameters[3:]:
                load.wait()
            prepare(0, "out")
            prepare(1, "in")
            prepare(1, "out")

        def gates(pair_of, carry):
            value = sigmoid(jnp.dot(gate_t[u], normed[pair_of], preferred_element_type=F32))
            gate[pair_of * 2] = value[:, :128]
            gate[pair_of * 2 + 1] = value[:, 128:]
            return carry

        lax.fori_loop(0, 18, gates, 0, unroll=2)

        for part in range(2):
            pltpu.make_async_copy(outgoing[part].at[0], incoming[part].at[0], own_sem.at[2 * u + part]).wait()

        def gather(group, carry):
            for part in range(2):
                arrival = recv_sem.at[(2 * u + part) * 8 + group]

                @pl.when(group == 0)
                def _():
                    blocks = incoming[part].at[pl.ds(0, 15)]
                    pltpu.make_async_copy(blocks, blocks, arrival).wait()

                @pl.when(group > 0)
                def _():
                    blocks = incoming[part].at[pl.ds(0, 16)]
                    pltpu.make_async_copy(blocks, blocks, arrival).wait()

            from_y, from_z = add_mod(y_lo, group, 2), add_mod(z_lo, lax.div(group, 2), 2)
            from_core = add_mod(core, lax.div(group, 4), 2)
            column = from_y * 4 + from_z * 2 + from_core
            for h in range(2):
                for hi in range(2):
                    for part in range(2):
                        turned = turn(
                            [incoming[part][(hi * 4 + at) * 16 + h * 8 + column].astype(F32) for at in range(4)]
                        )
                        for quarter in range(4):
                            for at, third, first, count in SEGMENTS[part]:
                                lanes = pl.ds((hi * 3 + third) * 128, 128)
                                to = pl.ds(h * 48 + quarter * 12 + first, count)
                                slab_left[to, lanes] = turned[quarter][at : at + count]
                                at += ROWS[part]
                                slab_right[to, lanes] = turned[quarter][at : at + count]
            if u == 0:
                left16[group] = slab_left[...].astype(BF16)
                for hi in range(2):
                    for third in range(3):
                        lanes = pl.ds((hi * 3 + third) * 128, 128)
                        flipped = slab_right[:, lanes].T.astype(BF16)
                        for at in range(4):
                            right_t[
                                pl.ds((hi * 4 + at) * 96 + third * 32, 32),
                                pl.ds(pl.multiple_of(group * 128, 128), 128),
                            ] = flipped[at * 32 : at * 32 + 32]
            else:
                for h in range(2):
                    right16[h * 8 + column] = slab_right[h * 48 : h * 48 + 48, :].astype(BF16)
                    for part in range(3):
                        sixth = from_core * 3 + part
                        to = h * 384 + lax.div(sixth, 2) * 128 + (from_y * 2 + from_z) * 32 + lax.rem(sixth, 2) * 16
                        at = h * 48 + part * 16
                        left16.reshape(1024, 768)[pl.ds(pl.multiple_of(to, 16), 16), :] = slab_left[
                            at : at + 16, :
                        ].astype(BF16)
            return carry

        lax.fori_loop(0, 8, gather, 0)

        if u == 1:
            for part in range(2):
                pltpu.make_async_copy(
                    sums_out[part].at[others], sums_out[part].at[others], sums_send_sem.at[part]
                ).wait()

        def columns_of(step):
            turn_y = lax.div(step, 2)
            to_y = add_mod(y, turn_y + 1 - 2 * lax.rem(turn_y, 2) + 2 * core, 4)
            return to_y * 2 + add_mod(z_lo, step, 2)

        def multiply(step, summed):
            rows_at = pl.ds(pl.multiple_of(columns_of(step) * 96, 96), 96)
            if u == 0:
                summed[...] = jnp.dot(
                    right_t[rows_at, :], left16.reshape(1024, 768)[...], preferred_element_type=F32
                )
            else:
                summed[...] = lax.dot_general(
                    right16.reshape(768, 768)[rows_at, :], left16.reshape(1024, 768)[0:768, :],
                    (((1,), (1,)), ((), ())), preferred_element_type=F32,
                )

        def send_back(step, part):
            pair_at = columns_of(step)

            def one(index, carry):
                s, to_row = pair_at * 2 + lax.div(index, 8), lax.rem(index, 8)
                to = to_row * 16 + s

                @pl.when(to != me)
                def _():
                    pltpu.make_async_remote_copy(
                        src_ref=sums_out[part].at[to], dst_ref=sums_in[part].at[my_channel],
                        send_sem=sums_send_sem.at[2 * u + part], recv_sem=sums_sem.at[2 * u + part],
                        device_id=(to_row, s), device_id_type=MESH,
                    ).start()

                @pl.when(to == me)
                def _():
                    pltpu.make_async_copy(
                        sums_out[part].at[to], sums_in[part].at[my_channel], own_sums_sem.at[2 * u + part]
                    ).start()

                return carry

            lax.fori_loop(0, 16, one, 0, unroll=4)

        def give_back(steps, carry):
            for parity, (summed, following) in enumerate(((summed0, summed1), (summed1, summed0))):
                step = steps * 2 + parity
                for to_core in range(2):
                    s = columns_of(step) * 2 + to_core
                    for hi in range(2):
                        for quarter in range(4):
                            for third in range(3):
                                piece[to_core * 2 + hi, quarter, third * 12 : third * 12 + 12, :] = summed[
                                    pl.ds(to_core * 48 + quarter * 12, 12), pl.ds((hi * 3 + third) * 128, 128)
                                ]
                for to_core in range(2):
                    s = columns_of(step) * 2 + to_core
                    for hi in range(2):
                        turned = turn([piece[to_core * 2 + hi, quarter] for quarter in range(4)])
                        for at in range(4):
                            to = (hi * 4 + at) * 16 + s
                            sums_out0[to] = turned[at][0:16].astype(BF16)
                            sums_out1[to] = turned[at][16:36].astype(BF16)
                multiply(lax.rem(step + 1, 8), following)
                send_back(step, 0)
            return carry

        multiply(0, summed0)
        lax.fori_loop(0, 4, give_back, 0)

        def give_rest(step, carry):
            send_back(step, 1)
            return carry

        lax.fori_loop(0, 8, give_rest, 0)

        for part in range(2):
            pltpu.make_async_copy(
                outgoing[part].at[others], outgoing[part].at[others], send_sem.at[2 * u + part]
            ).wait()

        def widen(part):
            pltpu.make_async_copy(
                sums_out[part].at[0], sums_in[part].at[0], own_sums_sem.at[2 * u + part]
            ).wait()
            pltpu.make_async_copy(
                sums_in[part].at[others], sums_in[part].at[others], sums_sem.at[2 * u + part]
            ).wait()

            def one(channel, carry):
                to = pl.ds(channel * WIDE + FIRST_ROW[part], ROWS[part])
                widened[to, :] = sums_in[part][channel].astype(F32)
                return carry

            lax.fori_loop(0, DEVICES, one, 0, unroll=8)

        def finish(pair_of, carry):
            mixed = []
            for half in range(2):
                values = widened[pl.ds(pair_of * 2 + half, 128, stride=WIDE), :]
                mixed.append(norm_columns(values, columns[u, 2], columns[u, 3]))
            update = jnp.dot(out_t[u], jnp.concatenate(mixed, axis=1), preferred_element_type=F32)
            halves = []
            for half in range(2):
                tile = pair_of * 2 + half
                values = state[tile] + gate[tile] * update[:, half * 128 : half * 128 + 128]
                if u == 0:
                    state[tile] = values
                    halves.append(norm_columns(values, columns[1, 0], columns[1, 1]))
                else:
                    tokens = values.T
                    for q in range(4):
                        rows[token_rows(tile, q), :] = tokens[q * 32 : q * 32 + 32]
            if u == 0:
                normed[pair_of] = jnp.concatenate(halves, axis=1)
            return carry

        widen(0)
        if u == 0:
            lax.fori_loop(0, 8, finish, 0, unroll=2)
            project_and_send(1, 0)
            widen(1)
            lax.fori_loop(8, 18, finish, 0, unroll=2)
            project_and_send(1, 1)
        else:
            stores = [
                pltpu.make_async_copy(
                    rows.at[pl.ds(i * 1536, 1536)], out.at[pl.ds(i * 1536, 1536)], copy_sem.at[i]
                )
                for i in range(3)
            ]
            lax.fori_loop(0, 6, finish, 0, unroll=2)
            stores[0].start()
            lax.fori_loop(6, 8, finish, 0, unroll=2)
            widen(1)
            lax.fori_loop(8, 12, finish, 0, unroll=2)
            stores[1].start()
            lax.fori_loop(12, 18, finish, 0, unroll=2)
            stores[2].start()

    for part in range(2):
        pltpu.make_async_copy(
            sums_out[part].at[others], sums_out[part].at[others], sums_send_sem.at[2 + part]
        ).wait()
    for store in stores:
        store.wait()


def local(pair, *parameters):
    anywhere = pl.BlockSpec(memory_space=pl.ANY)
    done = pl.pallas_call(
        kernel,
        out_shape=jax.ShapeDtypeStruct((4608, 128), F32),
        in_specs=[anywhere] * 8,
        out_specs=anywhere,
        scratch_shapes=[pltpu.VMEM(p.shape, p.dtype) for p in parameters] + [
            pltpu.VMEM((4608, 128), F32),
            pltpu.VMEM((36, 128, 128), F32),
            pltpu.VMEM((36, 128, 128), F32),
            pltpu.VMEM((18, 128, 256), BF16),
            pltpu.VMEM((16 * STRIDE + 8, 128), F32),
            pltpu.VMEM((128 * WIDE, 128), F32),
            pltpu.VMEM((128, 32, 128), BF16),
            pltpu.VMEM((128, 40, 128), BF16),
            pltpu.VMEM((128, 32, 128), BF16),
            pltpu.VMEM((128, 40, 128), BF16),
            pltpu.VMEM((128, 16, 128), BF16),
            pltpu.VMEM((128, 20, 128), BF16),
            pltpu.VMEM((128, 16, 128), BF16),
            pltpu.VMEM((128, 20, 128), BF16),
            pltpu.VMEM((128, 768), F32),
            pltpu.VMEM((128, 768), F32),
            pltpu.VMEM((8, 128, 768), BF16),
            pltpu.VMEM((16, 48, 768), BF16),
            pltpu.VMEM((768, 1024), BF16),
            pltpu.VMEM((96, 768), F32),
            pltpu.VMEM((96, 768), F32),
            pltpu.VMEM((4, 4, 36, 128), F32),
            pltpu.VMEM((2, 8, 64, 128), BF16),
            pltpu.VMEM((2, 128, 128), BF16),
            pltpu.VMEM((2, 128, 128), BF16),
            pltpu.VMEM((2, 4, 128, 128), F32),
            pltpu.SemaphoreType.DMA((3,)),
            pltpu.SemaphoreType.DMA((7,)),
            pltpu.SemaphoreType.DMA((4,)),
            pltpu.SemaphoreType.DMA((4,)),
            pltpu.SemaphoreType.DMA((4,)),
            pltpu.SemaphoreType.DMA((4,)),
            pltpu.SemaphoreType.DMA((32,)),
            pltpu.SemaphoreType.DMA((4,)),
            pltpu.SemaphoreType.REGULAR,
        ],
        compiler_params=pltpu.CompilerParams(
            collective_id=0, has_side_effects=True, vmem_limit_bytes=56 * 2**20
        ),
    )(pair.reshape(4608, 128), *parameters)
    return done.reshape(96, 48, 128)


def solution(mesh):
    return jax.shard_map(
        local,
        mesh=mesh,
        in_specs=(P("row", "col", None), P(), P(), P(), P(), P(), P(), P()),
        out_specs=P("row", "col", None),
        check_vma=False,
    )
```

time: 129 us -> 115 us (0.89)
  Pallas kernels: 125 us -> 112 us
    pallas_call x1, Pallas kernels: 125 us -> 112 us  [local(): pl.pallas_call(kernel, out_shape=jax.ShapeDtypeStruct((4608, 128), F32),...]
where the time goes in v3:
time: 115 us
  Pallas kernels  112 us (97%)
  local copies, waits for them, and re-layouts  3.22 us (3%)
    pallas_call x1, Pallas kernels, local(): pl.pallas_call(kernel, out_shape=jax.ShapeDtypeStruct((4608, 128), F32),...  112 us
    unnamed x1, local copies, waits for them, and re-layouts  3.22 us

profile of v3, /device:TPU:1, one launch (start us, length us, event | category | flops | bytes accessed | tf_op | source)
XLA Modules:
  0.0 115.2 jit_solution(13104030344070037622)
XLA Ops:
  0.0 112.0 %shard_map.82 = f32[4608,128]{1,0:T(8,128)} custom-call(f32[4608,128]{1,0:T(8,128)} %bitcast.3, f32[2,128]{1,0:T(2,128)} %in_gain_h.1, f32[2,128]{1,0:T(2,128)} %in_bias_h.1, f32[2,128]{1,0:T(2,128)} %mid_gain_h.1, f32[2,128]{1,0:T(2,128)} %mid_bias_h.1, bf16[2,128,512]{2,1,0:T(8,128)(2,1)} %w_in_h.1, bf16[2,128,128]{2,1,0:T(8,128)(2,1)} %w_gate_h.1, ...), custom_call_target="tpu_custom_call" | custom-call | tf_op jit(solution)/shard_map/pallas_call | solution.py:433
  112.0 3.2 %copy.10 = f32[96,48,128]{2,1,0:T(8,128)} copy(f32[96,48,128]{2,1,0:T(8,128)} %bitcast.2) | data formatting | bytes 4718592

commit v4 on v3

--- a/solution.py
+++ b/solution.py
@@ -12,7 +12,11 @@
 STRIDE = 41
 WIDE = 41
 FIRST_ROW, ROWS = (0, 16), (16, 20)
-SEGMENTS = (((0, 0, 0, 12), (12, 1, 0, 4)), ((0, 1, 4, 8), (8, 2, 0, 12)))
+RANGES = (((0, 8, 0, 16),), ((8, 12, 0, 8), (12, 18, 16, 12)))
+SEGMENTS = (
+    ((0, 16, 0, 0, 8), (8, 24, 1, 0, 8)),
+    ((0, 8, 2, 0, 8), (16, 28, 0, 8, 4), (20, 32, 1, 8, 4), (24, 36, 2, 8, 4)),
+)
 
 
 def add_mod(value, offset, size):
@@ -50,7 +54,7 @@
     in_gain, in_bias, mid_gain, mid_bias, w_in, w_gate, w_out,
     rows, state, gate, normed, staged, widened, outgoing0, outgoing1, incoming0, incoming1,
     sums_out0, sums_out1, sums_in0, sums_in1,
-    slab_left, slab_right, left16, right16, right_t, summed0, summed1, piece, weights, gate_t, out_t, columns,
+    slab_left, slab_right, flipped_rows, compact, left16, right16, right_t, summed0, summed1, weights, gate_t, out_t, columns,
     copy_sem, param_sem, own_sem, own_sums_sem, send_sem, sums_send_sem, recv_sem, sums_sem, plane_sem,
 ):
     row, col = lax.axis_index("row"), lax.axis_index("col")
@@ -80,19 +84,19 @@
     outgoing, incoming = (outgoing0, outgoing1), (incoming0, incoming1)
     sums_out, sums_in = (sums_out0, sums_out1), (sums_in0, sums_in1)
 
-    plane = [
-        device_at(add_mod(x, i, 4), add_mod(y, j, 4), z, core) for i in range(4) for j in range(4) if i + j
+    on_x, on_y, on_z = ([add_mod(at, i, 4) for i in range(4)] for at in (x, y, z))
+    same_core = [
+        device_at(on_x[i], on_y[j], on_z[k], core)
+        for i in (2, 1, 3, 0) for j in (2, 1, 3, 0) for k in (2, 1, 3, 0) if i + j + k
     ]
-    line = [
-        device_at(x, y, add_mod(z, i, 4), add_mod(core, j, 2)) for i in range(4) for j in range(2) if i + j
-    ]
+    other_core = [device_at(x, y, z, 1 - core)]
     barrier = pltpu.get_barrier_semaphore()
 
     def tell(semaphore, devices):
         for device in devices:
             pl.semaphore_signal(semaphore, inc=1, device_id=device, device_id_type=MESH)
 
-    tell(barrier, plane + line)
+    tell(barrier, same_core + other_core)
 
     def prepare(u, what):
         if what == "in":
@@ -113,7 +117,10 @@
     prepare(0, "in")
 
     def token_rows(tile, quarter):
-        start = lax.div(tile, 12) * 1536 + lax.rem(tile, 12) + quarter * 12
+        late = lax.div(tile, 24)
+        third = (1 - late) * lax.div(tile, 8) + late * lax.div(tile - 24 * late, 4)
+        b0 = (1 - late) * lax.rem(tile, 8) + late * (8 + lax.rem(tile, 4))
+        start = third * 1536 + b0 + quarter * 12
         return pl.ds(start, 32, stride=48)
 
     def enter(pair_of, carry):
@@ -128,54 +135,56 @@
         return carry
 
     loads[0].wait()
-    lax.fori_loop(0, 6, enter, 0, unroll=2)
-    pl.semaphore_wait(barrier, len(plane) + len(line))
-    tell(plane_sem, line)
+    lax.fori_loop(0, 4, enter, 0, unroll=2)
+    pl.semaphore_wait(barrier, 64)
+    tell(plane_sem, other_core)
     loads[1].wait()
-    lax.fori_loop(6, 8, enter, 0, unroll=2)
+    lax.fori_loop(4, 8, enter, 0, unroll=2)
 
     others = pl.ds(0, DEVICES - 1)
-    slab_left[96:128, :] = jnp.zeros((32, 768), F32)
-    slab_right[96:128, :] = jnp.zeros((32, 768), F32)
+    slab_left[...] = jnp.zeros((128, 768), F32)
+    slab_right[...] = jnp.zeros((128, 768), F32)
+    flipped_rows[...] = jnp.zeros((1024, 128), F32)
 
     def project_and_send(u, part):
-        base, count = FIRST_ROW[part], ROWS[part]
+        count = ROWS[part]
 
         def group_step(group, carry):
             to_y, to_z = add_mod(y_lo, group, 2), add_mod(z_lo, lax.div(group, 2), 2)
             to_core = add_mod(core, lax.div(group, 4), 2)
             which = to_y + to_z * 2 + to_core * 4
 
-            def project(pair_of, inner):
-                projected = jnp.dot(weights[u, which], normed[pair_of], preferred_element_type=F32)
-                for side in range(2):
-                    at = side * 32
-                    acts = sigmoid(projected[at : at + 16]) * projected[at + 16 : at + 32]
-                    for octet in range(2):
-                        for half in range(2):
-                            start = octet * 8 * STRIDE + side * count + pair_of * 2 + half - base
-                            staged[pl.ds(start, 8, stride=STRIDE), :] = acts[
-                                octet * 8 : octet * 8 + 8, half * 128 : half * 128 + 128
-                            ]
-                return inner
-
-            lax.fori_loop(base // 2, (base + count) // 2, project, 0, unroll=count // 4)
+            for first, last, row_at, side_step in RANGES[part]:
+
+                def project(pair_of, inner):
+                    projected = jnp.dot(weights[u, which], normed[pair_of], preferred_element_type=F32)
+                    for side in range(2):
+                        at = side * 32
+                        acts = sigmoid(projected[at : at + 16]) * projected[at + 16 : at + 32]
+                        for octet in range(2):
+                            for half in range(2):
+                                to = row_at + side * side_step + (pair_of - first) * 2 + half
+                                staged[pl.ds(octet * 8 * STRIDE + to, 8, stride=STRIDE), :] = acts[
+                                    octet * 8 : octet * 8 + 8, half * 128 : half * 128 + 128
+                                ]
+                    return inner
+
+                lax.fori_loop(first, last, project, 0, unroll=3 if last - first == 6 else 4)
 
             if u == 0 and part == 0:
                 @pl.when(group == 0)
                 def _():
-                    pl.semaphore_wait(plane_sem, len(line))
+                    pl.semaphore_wait(plane_sem, 1)
 
             def send(member, inner):
-                along = lax.rem(lax.div(member, 4) + lax.rem(member, 4) + 1, 4)
+                along = lax.rem(lax.div(member, 4) + lax.rem(member, 4), 4)
                 at_x = add_mod(x, along + core * (4 - 2 * along), 4)
                 at_y, at_z = add_mod(y_hi, member, 2), add_mod(z_hi, lax.div(member, 2), 2)
                 place = at_x + at_y * 4 + at_z * 8
                 channel = which * 16 + place
                 outgoing[part][channel] = staged[pl.ds(place * STRIDE, 2 * count), :].astype(BF16)
 
-                @pl.when(channel != my_channel)
-                def _():
+                def remote():
                     pltpu.make_async_remote_copy(
                         src_ref=outgoing[part].at[channel], dst_ref=incoming[part].at[me],
                         send_sem=send_sem.at[2 * u + part],
@@ -184,15 +193,20 @@
                         device_id_type=MESH,
                     ).start()
 
-                @pl.when(channel == my_channel)
-                def _():
-                    pltpu.make_async_copy(
-                        outgoing[part].at[channel], incoming[part].at[me], own_sem.at[2 * u + part]
-                    ).start()
-
+                if isinstance(member, int):
+                    pl.when(group > 0)(remote)
+
+                    @pl.when(group == 0)
+                    def _():
+                        pltpu.make_async_copy(
+                            outgoing[part].at[channel], incoming[part].at[me], own_sem.at[2 * u + part]
+                        ).start()
+                else:
+                    remote()
                 return inner
 
-            lax.fori_loop(0, 16, send, 0, unroll=4)
+            send(0, 0)
+            lax.fori_loop(1, 16, send, 0, unroll=15)
             return carry
 
         lax.fori_loop(0, 8, group_step, 0)
@@ -245,32 +259,38 @@
                             [incoming[part][(hi * 4 + at) * 16 + h * 8 + column].astype(F32) for at in range(4)]
                         )
                         for quarter in range(4):
-                            for at, third, first, count in SEGMENTS[part]:
+                            for left_at, right_at, third, first, count in SEGMENTS[part]:
                                 lanes = pl.ds((hi * 3 + third) * 128, 128)
-                                to = pl.ds(h * 48 + quarter * 12 + first, count)
-                                slab_left[to, lanes] = turned[quarter][at : at + count]
-                                at += ROWS[part]
-                                slab_right[to, lanes] = turned[quarter][at : at + count]
+                                to = pl.ds(h * 64 + quarter * 16 + first, count)
+                                slab_left[to, lanes] = turned[quarter][left_at : left_at + count]
+                                slab_right[to, lanes] = turned[quarter][right_at : right_at + count]
             if u == 0:
                 left16[group] = slab_left[...].astype(BF16)
                 for hi in range(2):
                     for third in range(3):
                         lanes = pl.ds((hi * 3 + third) * 128, 128)
-                        flipped = slab_right[:, lanes].T.astype(BF16)
+                        flipped = slab_right[:, lanes].T
                         for at in range(4):
-                            right_t[
-                                pl.ds((hi * 4 + at) * 96 + third * 32, 32),
-                                pl.ds(pl.multiple_of(group * 128, 128), 128),
-                            ] = flipped[at * 32 : at * 32 + 32]
+                            now, end = third * 32, third * 32 + 32
+                            while now < end:
+                                twelfth, within = now // 12, now % 12
+                                count = min(12 - within, end - now)
+                                to = (hi * 4 + at) * 128 + twelfth * 16 + within
+                                source = at * 32 + now - third * 32
+                                flipped_rows[to : to + count, :] = flipped[source : source + count]
+                                now += count
+                right_t[:, pl.ds(pl.multiple_of(group * 128, 128), 128)] = flipped_rows[...].astype(BF16)
             else:
                 for h in range(2):
-                    right16[h * 8 + column] = slab_right[h * 48 : h * 48 + 48, :].astype(BF16)
+                    right16[h * 8 + column] = slab_right[h * 64 : h * 64 + 64, :].astype(BF16)
+                    for quarter in range(4):
+                        at = h * 64 + quarter * 16
+                        compact[h, quarter * 12 : quarter * 12 + 12, :] = slab_left[at : at + 12, :]
                     for part in range(3):
                         sixth = from_core * 3 + part
                         to = h * 384 + lax.div(sixth, 2) * 128 + (from_y * 2 + from_z) * 32 + lax.rem(sixth, 2) * 16
-                        at = h * 48 + part * 16
-                        left16.reshape(1024, 768)[pl.ds(pl.multiple_of(to, 16), 16), :] = slab_left[
-                            at : at + 16, :
+                        left16.reshape(1024, 768)[pl.ds(pl.multiple_of(to, 16), 16), :] = compact[
+                            h, part * 16 : part * 16 + 16, :
                         ].astype(BF16)
             return carry
 
@@ -284,45 +304,52 @@
 
         def columns_of(step):
             turn_y = lax.div(step, 2)
-            to_y = add_mod(y, turn_y + 1 - 2 * lax.rem(turn_y, 2) + 2 * core, 4)
+            late = lax.div(turn_y, 2)
+            to_y = add_mod(y, (1 - late) * (2 - 2 * turn_y) + late * (2 * turn_y - 3) + 2 * core, 4)
             return to_y * 2 + add_mod(z_lo, step, 2)
 
         def multiply(step, summed):
-            rows_at = pl.ds(pl.multiple_of(columns_of(step) * 96, 96), 96)
+            rows_at = pl.ds(pl.multiple_of(columns_of(step) * 128, 128), 128)
             if u == 0:
                 summed[...] = jnp.dot(
                     right_t[rows_at, :], left16.reshape(1024, 768)[...], preferred_element_type=F32
                 )
             else:
                 summed[...] = lax.dot_general(
-                    right16.reshape(768, 768)[rows_at, :], left16.reshape(1024, 768)[0:768, :],
+                    right16.reshape(1024, 768)[rows_at, :], left16.reshape(1024, 768)[0:768, :],
                     (((1,), (1,)), ((), ())), preferred_element_type=F32,
                 )
 
         def send_back(step, part):
             pair_at = columns_of(step)
 
-            def one(index, carry):
-                s, to_row = pair_at * 2 + lax.div(index, 8), lax.rem(index, 8)
+            def one(member, carry):
+                to_x = add_mod(x, lax.div(member, 4) + lax.rem(member, 4), 4)
+                to_row = add_mod(z_hi, member, 2) * 4 + to_x
+                s = pair_at * 2 + add_mod(core, lax.div(member, 2), 2)
                 to = to_row * 16 + s
 
-                @pl.when(to != me)
-                def _():
+                def remote():
                     pltpu.make_async_remote_copy(
                         src_ref=sums_out[part].at[to], dst_ref=sums_in[part].at[my_channel],
                         send_sem=sums_send_sem.at[2 * u + part], recv_sem=sums_sem.at[2 * u + part],
                         device_id=(to_row, s), device_id_type=MESH,
                     ).start()
 
-                @pl.when(to == me)
-                def _():
-                    pltpu.make_async_copy(
-                        sums_out[part].at[to], sums_in[part].at[my_channel], own_sums_sem.at[2 * u + part]
-                    ).start()
-
+                if isinstance(member, int):
+                    pl.when(to != me)(remote)
+
+                    @pl.when(to == me)
+                    def _():
+                        pltpu.make_async_copy(
+                            sums_out[part].at[to], sums_in[part].at[my_channel], own_sums_sem.at[2 * u + part]
+                        ).start()
+                else:
+                    remote()
                 return carry
 
-            lax.fori_loop(0, 16, one, 0, unroll=4)
+            one(0, 0)
+            lax.fori_loop(1, 16, one, 0, unroll=15)
 
         def give_back(steps, carry):
             for parity, (summed, following) in enumerate(((summed0, summed1), (summed1, summed0))):
@@ -330,19 +357,23 @@
                 for to_core in range(2):
                     s = columns_of(step) * 2 + to_core
                     for hi in range(2):
-                        for quarter in range(4):
-                            for third in range(3):
-                                piece[to_core * 2 + hi, quarter, third * 12 : third * 12 + 12, :] = summed[
-                                    pl.ds(to_core * 48 + quarter * 12, 12), pl.ds((hi * 3 + third) * 128, 128)
+                        for part in range(2):
+                            blocks = []
+                            for quarter in range(4):
+                                at = to_core * 64 + quarter * 16
+                                pieces = [
+                                    summed[pl.ds(at + first, count), pl.ds((hi * 3 + third) * 128, 128)]
+                                    for _, _, third, first, count in SEGMENTS[part]
                                 ]
-                for to_core in range(2):
-                    s = columns_of(step) * 2 + to_core
-                    for hi in range(2):
-                        turned = turn([piece[to_core * 2 + hi, quarter] for quarter in range(4)])
-                        for at in range(4):
-                            to = (hi * 4 + at) * 16 + s
-                            sums_out0[to] = turned[at][0:16].astype(BF16)
-                            sums_out1[to] = turned[at][16:36].astype(BF16)
+                                blocks.append(jnp.concatenate(pieces, axis=0))
+                            turned = turn(blocks)
+                            for at in range(4):
+                                to = (hi * 4 + at) * 16 + s
+                                if part == 0:
+                                    sums_out0[to] = turned[at].astype(BF16)
+                                else:
+                                    for four in range(5):
+                                        sums_out1[to, four] = turned[at][four * 4 : four * 4 + 4].astype(BF16)
                 multiply(lax.rem(step + 1, 8), following)
                 send_back(step, 0)
             return carry
@@ -370,8 +401,12 @@
             ).wait()
 
             def one(channel, carry):
-                to = pl.ds(channel * WIDE + FIRST_ROW[part], ROWS[part])
-                widened[to, :] = sums_in[part][channel].astype(F32)
+                to = channel * WIDE + FIRST_ROW[part]
+                if part == 0:
+                    widened[pl.ds(to, 16), :] = sums_in0[channel].astype(F32)
+                else:
+                    for four in range(5):
+                        widened[pl.ds(to + four * 4, 4), :] = sums_in1[channel, four].astype(F32)
                 return carry
 
             lax.fori_loop(0, DEVICES, one, 0, unroll=8)
@@ -411,13 +446,13 @@
                 )
                 for i in range(3)
             ]
-            lax.fori_loop(0, 6, finish, 0, unroll=2)
+            lax.fori_loop(0, 8, finish, 0, unroll=2)
+            widen(1)
+            lax.fori_loop(8, 14, finish, 0, unroll=2)
             stores[0].start()
-            lax.fori_loop(6, 8, finish, 0, unroll=2)
-            widen(1)
-            lax.fori_loop(8, 12, finish, 0, unroll=2)
+            lax.fori_loop(14, 16, finish, 0, unroll=2)
             stores[1].start()
-            lax.fori_loop(12, 18, finish, 0, unroll=2)
+            lax.fori_loop(16, 18, finish, 0, unroll=2)
             stores[2].start()
 
     for part in range(2):
@@ -447,17 +482,18 @@
             pltpu.VMEM((128, 32, 128), BF16),
             pltpu.VMEM((128, 40, 128), BF16),
             pltpu.VMEM((128, 16, 128), BF16),
-            pltpu.VMEM((128, 20, 128), BF16),
+            pltpu.VMEM((128, 5, 4, 128), BF16),
             pltpu.VMEM((128, 16, 128), BF16),
-            pltpu.VMEM((128, 20, 128), BF16),
+            pltpu.VMEM((128, 5, 4, 128), BF16),
             pltpu.VMEM((128, 768), F32),
             pltpu.VMEM((128, 768), F32),
+            pltpu.VMEM((1024, 128), F32),
+            pltpu.VMEM((2, 48, 768), F32),
             pltpu.VMEM((8, 128, 768), BF16),
-            pltpu.VMEM((16, 48, 768), BF16),
-            pltpu.VMEM((768, 1024), BF16),
-            pltpu.VMEM((96, 768), F32),
-            pltpu.VMEM((96, 768), F32),
-            pltpu.VMEM((4, 4, 36, 128), F32),
+            pltpu.VMEM((16, 64, 768), BF16),
+            pltpu.VMEM((1024, 1024), BF16),
+            pltpu.VMEM((128, 768), F32),
+            pltpu.VMEM((128, 768), F32),
             pltpu.VMEM((2, 8, 64, 128), BF16),
             pltpu.VMEM((2, 128, 128), BF16),
             pltpu.VMEM((2, 128, 128), BF16),

time: 115 us -> 112 us (0.974)
  Pallas kernels: 112 us -> 109 us
    pallas_call x1, Pallas kernels: 112 us -> 109 us  [local(): pl.pallas_call(kernel, out_shape=jax.ShapeDtypeStruct((4608, 128), F32),...]
where the time goes in v4:
time: 112 us
  Pallas kernels  109 us (97%)
  local copies, waits for them, and re-layouts  3.22 us (3%)
    pallas_call x1, Pallas kernels, local(): pl.pallas_call(kernel, out_shape=jax.ShapeDtypeStruct((4608, 128), F32),...  109 us
    unnamed x1, local copies, waits for them, and re-layouts  3.22 us

profile of v4, /device:TPU:1, one launch (start us, length us, event | category | flops | bytes accessed | tf_op | source)
XLA Modules:
  0.0 112.0 jit_solution(9990025266138710992)
XLA Ops:
  0.0 108.8 %shard_map.82 = f32[4608,128]{1,0:T(8,128)} custom-call(f32[4608,128]{1,0:T(8,128)} %bitcast.3, f32[2,128]{1,0:T(2,128)} %in_gain_h.1, f32[2,128]{1,0:T(2,128)} %in_bias_h.1, f32[2,128]{1,0:T(2,128)} %mid_gain_h.1, f32[2,128]{1,0:T(2,128)} %mid_bias_h.1, bf16[2,128,512]{2,1,0:T(8,128)(2,1)} %w_in_h.1, bf16[2,128,128]{2,1,0:T(8,128)(2,1)} %w_gate_h.1, ...), custom_call_target="tpu_custom_call" | custom-call | tf_op jit(solution)/shard_map/pallas_call | solution.py:468
  108.8 3.2 %copy.10 = f32[96,48,128]{2,1,0:T(8,128)} copy(f32[96,48,128]{2,1,0:T(8,128)} %bitcast.2) | data formatting | bytes 4718592

commit v5 on v4

--- a/solution.py
+++ b/solution.py
@@ -25,6 +25,13 @@
 
 def device_at(x, y, z, core):
     return lax.div(z, 2) * 4 + x, y * 4 + lax.rem(z, 2) * 2 + core
+
+
+def offset_along(member, ending):
+    quad = lax.div(member, 4)
+    late = lax.div(quad, 2)
+    far = (1 - late) * (2 - quad) + late * (9 - 3 * quad)
+    return (1 - ending) * lax.rem(quad + lax.rem(member, 4), 4) + ending * far
 
 
 def sigmoid(values):
@@ -177,7 +184,7 @@
                     pl.semaphore_wait(plane_sem, 1)
 
             def send(member, inner):
-                along = lax.rem(lax.div(member, 4) + lax.rem(member, 4), 4)
+                along = offset_along(member, lax.div(group, 7) * part)
                 at_x = add_mod(x, along + core * (4 - 2 * along), 4)
                 at_y, at_z = add_mod(y_hi, member, 2), add_mod(z_hi, lax.div(member, 2), 2)
                 place = at_x + at_y * 4 + at_z * 8
@@ -324,7 +331,7 @@
             pair_at = columns_of(step)
 
             def one(member, carry):
-                to_x = add_mod(x, lax.div(member, 4) + lax.rem(member, 4), 4)
+                to_x = add_mod(x, offset_along(member, lax.div(step, 7) * part), 4)
                 to_row = add_mod(z_hi, member, 2) * 4 + to_x
                 s = pair_at * 2 + add_mod(core, lax.div(member, 2), 2)
                 to = to_row * 16 + s
@@ -351,41 +358,45 @@
             one(0, 0)
             lax.fori_loop(1, 16, one, 0, unroll=15)
 
-        def give_back(steps, carry):
-            for parity, (summed, following) in enumerate(((summed0, summed1), (summed1, summed0))):
-                step = steps * 2 + parity
-                for to_core in range(2):
-                    s = columns_of(step) * 2 + to_core
-                    for hi in range(2):
-                        for part in range(2):
-                            blocks = []
-                            for quarter in range(4):
-                                at = to_core * 64 + quarter * 16
-                                pieces = [
-                                    summed[pl.ds(at + first, count), pl.ds((hi * 3 + third) * 128, 128)]
-                                    for _, _, third, first, count in SEGMENTS[part]
-                                ]
-                                blocks.append(jnp.concatenate(pieces, axis=0))
-                            turned = turn(blocks)
-                            for at in range(4):
-                                to = (hi * 4 + at) * 16 + s
-                                if part == 0:
-                                    sums_out0[to] = turned[at].astype(BF16)
-                                else:
-                                    for four in range(5):
-                                        sums_out1[to, four] = turned[at][four * 4 : four * 4 + 4].astype(BF16)
-                multiply(lax.rem(step + 1, 8), following)
-                send_back(step, 0)
+        def spread(step, part, summed):
+            for to_core in range(2):
+                s = columns_of(step) * 2 + to_core
+                for hi in range(2):
+                    blocks = []
+                    for quarter in range(4):
+                        at = to_core * 64 + quarter * 16
+                        pieces = [
+                            summed[pl.ds(at + first, count), pl.ds((hi * 3 + third) * 128, 128)]
+                            for _, _, third, first, count in SEGMENTS[part]
+                        ]
+                        blocks.append(jnp.concatenate(pieces, axis=0))
+                    turned = turn(blocks)
+                    for at in range(4):
+                        to = (hi * 4 + at) * 16 + s
+                        if part == 0:
+                            sums_out0[to] = turned[at].astype(BF16)
+                        else:
+                            for four in range(5):
+                                sums_out1[to, four] = turned[at][four * 4 : four * 4 + 4].astype(BF16)
+
+        def give_first(steps, carry):
+            spread(steps * 2, 0, summed0.at[steps])
+            multiply(steps * 2 + 1, summed1.at[steps])
+            send_back(steps * 2, 0)
+            spread(steps * 2 + 1, 0, summed1.at[steps])
+            multiply(lax.rem(steps * 2 + 2, 8), summed0.at[lax.rem(steps + 1, 4)])
+            send_back(steps * 2 + 1, 0)
             return carry
 
-        multiply(0, summed0)
-        lax.fori_loop(0, 4, give_back, 0)
-
-        def give_rest(step, carry):
-            send_back(step, 1)
+        def give_rest(steps, carry):
+            for parity, summed in enumerate((summed0, summed1)):
+                spread(steps * 2 + parity, 1, summed.at[steps])
+                send_back(steps * 2 + parity, 1)
             return carry
 
-        lax.fori_loop(0, 8, give_rest, 0)
+        multiply(0, summed0.at[0])
+        lax.fori_loop(0, 4, give_first, 0)
+        lax.fori_loop(0, 4, give_rest, 0)
 
         for part in range(2):
             pltpu.make_async_copy(
@@ -492,8 +503,8 @@
             pltpu.VMEM((8, 128, 768), BF16),
             pltpu.VMEM((16, 64, 768), BF16),
             pltpu.VMEM((1024, 1024), BF16),
-            pltpu.VMEM((128, 768), F32),
-            pltpu.VMEM((128, 768), F32),
+            pltpu.VMEM((4, 128, 768), F32),
+            pltpu.VMEM((4, 128, 768), F32),
             pltpu.VMEM((2, 8, 64, 128), BF16),
             pltpu.VMEM((2, 128, 128), BF16),
             pltpu.VMEM((2, 128, 128), BF16),

time: 112 us -> 111 us (level)
  no operation moved by 1% of the time
where the time goes in v5:
time: 111 us
  Pallas kernels  108 us (97%)
  local copies, waits for them, and re-layouts  3.22 us (3%)
    pallas_call x1, Pallas kernels, local(): pl.pallas_call(kernel, out_shape=jax.ShapeDtypeStruct((4608, 128), F32),...  108 us
    unnamed x1, local copies, waits for them, and re-layouts  3.22 us

profile of v5, /device:TPU:1, one launch (start us, length us, event | category | flops | bytes accessed | tf_op | source)
XLA Modules:
  0.0 111.1 jit_solution(10556145189521844583)
XLA Ops:
  0.0 107.9 %shard_map.82 = f32[4608,128]{1,0:T(8,128)} custom-call(f32[4608,128]{1,0:T(8,128)} %bitcast.3, f32[2,128]{1,0:T(2,128)} %in_gain_h.1, f32[2,128]{1,0:T(2,128)} %in_bias_h.1, f32[2,128]{1,0:T(2,128)} %mid_gain_h.1, f32[2,128]{1,0:T(2,128)} %mid_bias_h.1, bf16[2,128,512]{2,1,0:T(8,128)(2,1)} %w_in_h.1, bf16[2,128,128]{2,1,0:T(8,128)(2,1)} %w_gate_h.1, ...), custom_call_target="tpu_custom_call" | custom-call | tf_op jit(solution)/shard_map/pallas_call | solution.py:479
  107.9 3.2 %copy.10 = f32[96,48,128]{2,1,0:T(8,128)} copy(f32[96,48,128]{2,1,0:T(8,128)} %bitcast.2) | data formatting | bytes 4718592
